TPU v7x, 512 devices: a whole 4x8x8 slice. The times are simulated.
512 devices in a mesh: dom: 64 (over y, x, core), ao: 8 (over z).
Axes of the slice: x: 4, y: 8, z: 8, core: 2. Of those that a mesh axis runs over, the one named last changes fastest.
Arguments:
- three_index: bfloat16 [512, 256, 4096], P('dom', None, 'ao'), may hold values from -1.5 to 1.5
- occ_coef: bfloat16 [4096, 1024], P('ao'), may hold values from -0.09375 to 0.09375
- pao_coef: bfloat16 [512, 4096, 128], P(('dom', 'ao')), may hold values from -0.375 to 0.375
- ao_map: int32 [512, 256], P(('dom', 'ao')), may hold values 0 or 1
- aux_map: int32 [512, 4], P(('dom', 'ao')), may hold values 0 or 1
- ao_list: int32 [4, 16], replicated, may hold values from 0 to 255, as said below
Outputs:
- pair_self: bfloat16 [512, 256, 256], P(('dom', 'ao'))
- pair_near: bfloat16 [512, 256, 256], P(('dom', 'ao'))
Inputs may be any that keep to these rules, and one draw needn't show every extreme that they name: `ao_list`: each row names 16 different AO shell blocks.
All inputs are finite; a program needn't handle non-finite values. No bound on the sum of `ao_map` or of `aux_map` on one device may be relied on, other than what follows from the above.
Results may differ from a plain program's by a relative error of at most 0.029.
Values may be sent and summed in bfloat16 or wider, within the bound.
No kernel may reach another device: no remote copies, remote signals or barrier semaphores. Data moves between devices by JAX's collectives and lax.ppermute only.
A program may use at most 64 MiB of HBM per device.

v0:
```python
import jax
import jax.numpy as jnp
from jax import lax
from jax.sharding import PartitionSpec as P

QB = 128
NU = 4096
AOB = 16
OCC_D = 2
PAO_D = 128


def from_behind(value, axis, steps):
    count = lax.axis_size(axis)
    pairs = [(source, (source + steps) % count) for source in range(count)]
    return lax.ppermute(value, axis, pairs)


def body(three_index, occ_coef, pao_coef, ao_map, aux_map, ao_list):
    dom_count = lax.axis_size("dom")
    ao_count = lax.axis_size("ao")
    aux_rows, mu_rows, nu_local = three_index.shape
    blocks = ao_list.shape[0]
    occ_four = occ_coef.reshape(nu_local, dom_count, ao_count, OCC_D)
    span_count = dom_count * lax.axis_size("ao") // dom_count
    term_block = jnp.einsum(
        "qmn,ngro->rgqom", three_index, occ_four, preferred_element_type=jnp.float32
    )
    summed = lax.psum_scatter(
        term_block.reshape(span_count * dom_count, aux_rows, OCC_D, mu_rows).astype(jnp.bfloat16),
        "ao",
        scatter_dimension=0,
        tiled=True,
    )
    pao_shells = pao_coef[0].reshape(NU // AOB, AOB, PAO_D)
    masked = pao_shells * ao_map[0].astype(jnp.bfloat16)[:, None, None]
    projector = masked[ao_list].reshape(blocks, mu_rows, PAO_D)
    aux_keep = jnp.repeat(aux_map[0], QB).astype(jnp.bfloat16)
    total_aux = aux_rows * dom_count
    arrived = lax.all_to_all(summed, "dom", split_axis=0, concat_axis=1, tiled=True)
    shaped = arrived.reshape(total_aux, OCC_D, mu_rows).reshape(blocks, QB, OCC_D, mu_rows)
    result = jnp.einsum("bqkm,bma->bqka", shaped, projector, preferred_element_type=jnp.float32)
    full_ints = result.astype(jnp.bfloat16).reshape(total_aux, OCC_D * projector.shape[2])
    near_ints = from_behind(full_ints, "dom", 1)
    fitted = full_ints * aux_keep[:, None]
    pair_self = jnp.einsum("qx,qy->xy", fitted, full_ints, preferred_element_type=jnp.float32)
    pair_near = jnp.einsum("qx,qy->xy", fitted, near_ints, preferred_element_type=jnp.float32)
    return (pair_self.astype(jnp.bfloat16)[None], pair_near.astype(jnp.bfloat16)[None])


def solution(mesh):
    placed = (
        P("dom", None, "ao"),
        P("ao", None),
        P(("dom", "ao"), None, None),
        P(("dom", "ao"), None),
        P(("dom", "ao"), None),
        P(),
    )
    return jax.shard_map(
        body,
        mesh=mesh,
        in_specs=placed,
        out_specs=(P(("dom", "ao"), None, None), P(("dom", "ao"), None, None)),
        check_vma=False,
    )
```

profile of v0, /device:TPU:16, one launch (start us, length us, event | category | flops | bytes accessed | tf_op | source)
XLA Modules:
  0.0 126.3 jit_solution(8420403501274203280)
XLA Ops:
  7.2 0.0 copy-start
  7.2 0.0 reduce-scatter.2.cloned.1.call-start
  7.2 1.6 %copy.9 = bf16[512,1024]{0,1:T(8,128)(2,1)S(1)} copy(bf16[512,1024]{1,0:T(8,128)(2,1)} %param.7) | data formatting | bytes 2097152 | tf_op args[1]
  8.9 1.2 reshape.40
  10.1 0.0 copy-done
  10.1 3.6 %convert_bitcast_fusion = bf16[8,64,8,2,256]{4,0,2,3,1:T(8,128)(2,1)S(1)} fusion(bf16[8,256,512]{2,1,0:T(8,128)(2,1)S(1)} %copy-done, bf16[512,64,8,2,1]{0,3,2,1,4:T(2,128)(2,1)} %bitcast.44), kind=kOutput, calls=%fused_computation.1 | convolution fusion | flops 2149580800 | bytes 7340032 | tf_op jit(solution)/shard_map/qmn,ngro->rgqom/dot_general | solution.py:26
  13.7 2.8 %copy.11 = bf16[8,64,8,2,256]{4,2,3,1,0:T(8,128)(2,1)} copy(bf16[8,64,8,2,256]{4,0,2,3,1:T(8,128)(2,1)S(1)} %convert_bitcast_fusion) | data formatting | bytes 8388608 | tf_op jit(solution)/shard_map/convert_element_type | solution.py:30
  16.5 0.0 copy-start.1
  16.5 0.0 copy-start.2
  16.5 0.0 copy-start.3
  16.5 0.0 reduce-scatter.2.cloned.1.call-update
  16.5 63.4 %reduce-scatter.2.cloned.1.call-done = bf16[64,8,2,256]{3,1,2,0:T(8,128)(2,1)} async-done(((bf16[512,8,2,256]{3,1,2,0:T(8,128)(2,1)}), bf16[64,8,2,256]{3,1,2,0:T(8,128)(2,1)}) %reduce-scatter.2.cloned.1.call-update) | async-done | bytes 524304 | tf_op jit(solution)/shard_map/reduce_scatter | solution.py:29
  79.8 10.2 %all-to-all-start = ((bf16[64,8,2,256]{3,1,2,0:T(8,128)(2,1)}), bf16[64,8,2,256]{3,1,2,0:T(8,128)(2,1)S(1)}, u32[]{:S(2)}, u32[]{:S(2)}) async-start(bf16[64,8,2,256]{3,1,2,0:T(8,128)(2,1)} %reduce-scatter.2.cloned.1.call-done), calls=%async_computation.1 | async-start | bytes 1048576 | tf_op jit(solution)/shard_map/all_to_all | solution.py:40
  90.1 0.0 copy-done.1
  90.1 0.1 reshape.45
  90.2 0.0 copy-done.2
  90.2 2.5 %broadcast_multiply_fusion = bf16[256,16,128]{2,1,0:T(8,128)(2,1)} fusion(bf16[256,16,128]{2,1,0:T(8,128)(2,1)} %bitcast.43, bf16[256]{0:T(256)(128)(2,1)S(1)} %convert_reduce_fusion), kind=kLoop, calls=%fused_computation.10 | loop fusion | flops 524288 | bytes 2097664 | tf_op jit(solution)/shard_map/mul | solution.py:36
  92.8 1.9 %gather_fusion = bf16[64,16,128]{2,1,0:T(8,128)(2,1)S(1)} fusion(bf16[256,16,128]{2,1,0:T(8,128)(2,1)} %broadcast_multiply_fusion, s32[1024]{0:T(1024)S(1)} %pad_clamp_fusion), kind=kCustom, calls=%fused_computation | custom fusion | bytes 524544 | tf_op jit(solution)/shard_map/gather | solution.py:37
  94.6 0.0 copy-done.3
  94.6 13.3 %all-to-all-done = bf16[64,8,2,256]{3,1,2,0:T(8,128)(2,1)S(1)} async-done(((bf16[64,8,2,256]{3,1,2,0:T(8,128)(2,1)}), bf16[64,8,2,256]{3,1,2,0:T(8,128)(2,1)S(1)}, u32[]{:S(2)}, u32[]{:S(2)}) %all-to-all-start) | async-done | bytes 524320 | tf_op jit(solution)/shard_map/all_to_all | solution.py:40
  108.0 0.3 broadcast_multiply_fusion.1
  108.3 0.3 copy.15
  108.6 1.9 %collective-permute-start = (bf16[512,256]{1,0:T(8,128)(2,1)S(1)}, bf16[512,256]{1,0:T(8,128)(2,1)S(1)}, u32[]{:S(2)}, u32[]{:S(2)}) collective-permute-start(bf16[512,256]{1,0:T(8,128)(2,1)S(1)} %bitcast.50), channel_id=1, source_target_pairs={{0,8},{8,16},{16,24},{24,32},{32,40},{40,48},{48,56},{56,64},{64,7... | collective-permute-start | bytes 786440 | tf_op jit(solution)/shard_map/ppermute | solution.py:16
  110.5 0.1 broadcast_bitcast_fusion
  110.6 0.3 copy.14
  110.9 0.9 fusion.1
  111.8 6.6 %collective-permute-done = bf16[512,256]{1,0:T(8,128)(2,1)S(1)} collective-permute-done((bf16[512,256]{1,0:T(8,128)(2,1)S(1)}, bf16[512,256]{1,0:T(8,128)(2,1)S(1)}, u32[]{:S(2)}, u32[]{:S(2)}) %collective-permute-start) | collective-permute-done | bytes 262176 | tf_op jit(solution)/shard_map/ppermute | solution.py:16
  118.4 1.1 fusion.2
  (6 shorter events, 0.1 us)
Async XLA Ops:
  7.2 2.9 %copy-start = (bf16[8,256,512]{2,1,0:T(8,128)(2,1)S(1)}, bf16[8,256,512]{2,1,0:T(8,128)(2,1)}, u32[]{:S(2)}) copy-start(bf16[8,256,512]{2,1,0:T(8,128)(2,1)} %param.6) | copy-start | bytes 6291460
  7.2 72.7 %reduce-scatter.2.cloned.1.call-start = ((), (), s32[]{:S(2)}) async-start(), calls=%async_computation.2 | async-start | bytes 4718592 | tf_op jit(solution)/shard_map/reduce_scatter | solution.py:29
  16.5 73.6 %copy-start.1 = (s32[4,16]{1,0:T(4,128)S(1)}, s32[4,16]{1,0:T(4,128)}, u32[]{:S(2)}) copy-start(s32[4,16]{1,0:T(4,128)} %param.11) | copy-start | bytes 772
  16.5 73.7 %copy-start.2 = (s32[1,256]{1,0:T(1,128)S(1)}, s32[1,256]{1,0:T(1,128)}, u32[]{:S(2)}) copy-start(s32[1,256]{1,0:T(1,128)} %param.9) | copy-start | bytes 3076
  16.5 78.2 %copy-start.3 = (s32[1,4]{1,0:T(1,128)S(1)}, s32[1,4]{1,0:T(1,128)}, u32[]{:S(2)}) copy-start(s32[1,4]{1,0:T(1,128)} %param.10) | copy-start | bytes 52
  79.8 28.1 %all-to-all-start = ((bf16[64,8,2,256]{3,1,2,0:T(8,128)(2,1)}), bf16[64,8,2,256]{3,1,2,0:T(8,128)(2,1)S(1)}, u32[]{:S(2)}, u32[]{:S(2)}) async-start(bf16[64,8,2,256]{3,1,2,0:T(8,128)(2,1)} %reduce-scatter.2.cloned.1.call-done), calls=%async_computation.1 | async-start | bytes 1048576 | tf_op jit(solution)/shard_map/all_to_all | solution.py:40
  108.6 9.8 %collective-permute-start = (bf16[512,256]{1,0:T(8,128)(2,1)S(1)}, bf16[512,256]{1,0:T(8,128)(2,1)S(1)}, u32[]{:S(2)}, u32[]{:S(2)}) collective-permute-start(bf16[512,256]{1,0:T(8,128)(2,1)S(1)} %bitcast.50), channel_id=1, source_target_pairs={{0,8},{8,16},{16,24},{24,32},{32,40},{40,48},{48,56},{56,64},{64,7... | collective-permute-start | bytes 786440 | tf_op jit(solution)/shard_map/ppermute | solution.py:16
Sparse Core Ops, SparseCore 0:
  16.6 63.1 reduce-scatter.1
where the time goes:
time: 127 us; the launch traced here: 126 us
  waiting for transfers between devices  83.2 us (66%)
  between operations  14.1 us (11%)
  starting transfers between devices  12.2 us (10%)
  local copies, waits for them, and re-layouts  8.27 us (7%)
  matrix products  5.87 us (5%)
  other arithmetic  2.58 us (2%)
    reduce_scatter x1, waiting for transfers between devices, body(): lax.psum_scatter(term_block.reshape(span_count * dom_count, aux_rows, OCC...  63.4 us
    all_to_all x1, waiting for transfers between devices, body(): lax.all_to_all(summed, 'dom', split_axis=0, concat_axis=1, tiled=True)  13.3 us
    all_to_all x1, starting transfers between devices, body(): lax.all_to_all(summed, 'dom', split_axis=0, concat_axis=1, tiled=True)  10.2 us
    ppermute x1, waiting for transfers between devices, from_behind(): return lax.ppermute(value, axis, pairs)  6.59 us
    dot_general x1, matrix products, body(): jnp.einsum('qmn,ngro->rgqom', three_index, occ_four, preferred_element_ty...  3.59 us
    convert_element_type x1, local copies, waits for them, and re-layouts, body(): term_block.reshape(span_count * dom_count, aux_rows, OCC_D, mu_rows)  2.77 us
  transfers between devices with their start and end apart: 3, of which 3 were waited for; matrix products, arithmetic and copies ran while one was open for 5% of the time, Pallas kernels for 0%

commit v1 on v0

v1 whole, which is shorter than its diff:
```python
import functools

import jax
import jax.numpy as jnp
from jax import lax
from jax.experimental import pallas as pl
from jax.experimental.pallas import tpu as pltpu
from jax.sharding import PartitionSpec as P

QB = 128
AOB = 16
OCC_D = 2
BF = jnp.bfloat16
F32 = jnp.float32
PARTS = 1
FIRST_VMEM = 56 * 2**20
VMEM_LIMIT = 16 * 2**20


def hop(value, doms, ring):
    pairs = []
    for d in range(doms):
        step = 1 if d % 2 == 0 else -1
        for s in range(ring):
            pairs.append((d * ring + s, d * ring + (s + step) % ring))
    return lax.ppermute(value, ("dom", "ao"), pairs)


def swap(value, doms):
    return lax.ppermute(value, "dom", [(d, d ^ 1) for d in range(doms)])


def nt(x, y):
    return lax.dot_general(x, y, (((1,), (1,)), ((), ())), preferred_element_type=F32)


def pick_rows(occ, rows, ring, ahead):
    way = 1 - 2 * (lax.axis_index("dom") % 2)
    shard = (lax.axis_index("ao") + ahead * way + ring) % ring
    row = lax.broadcasted_iota(jnp.int32, (rows, occ.shape[1]), 0)
    col = lax.broadcasted_iota(jnp.int32, (rows, occ.shape[1]), 1)
    home = (row // OCC_D) * (ring * OCC_D) + row % OCC_D + shard * OCC_D
    pick = jnp.where(col == home, 1.0, 0.0).astype(BF)
    return nt(pick, occ).astype(BF)


def first_kernel(ring, occ_hbm, slab_hbm, *refs):
    out_refs = refs[:PARTS]
    occ_ref, slab_ref, occ_sem, slab_sems = refs[PARTS:]
    cut = slab_ref.shape[0] // PARTS
    occ_copy = pltpu.make_async_copy(occ_hbm, occ_ref, occ_sem)
    occ_copy.start()
    slab_copies = []
    for c in range(PARTS):
        part = pl.ds(c * cut, cut)
        slab_copies.append(pltpu.make_async_copy(slab_hbm.at[part], slab_ref.at[part], slab_sems.at[c]))
        slab_copies[-1].start()
    occ_copy.wait()
    w = pick_rows(occ_ref[...], out_refs[0].shape[0], ring, ring // 2)
    for c in range(PARTS):
        slab_copies[c].wait()
        out_refs[c][...] = nt(w, slab_ref[c * cut : (c + 1) * cut]).astype(BF)


def first_term(occ, slab, ring):
    rows, width = occ.shape[1] // ring, slab.shape[0] // PARTS
    vm, hbm = pl.BlockSpec(memory_space=pltpu.VMEM), pl.BlockSpec(memory_space=pl.ANY)
    return pl.pallas_call(
        functools.partial(first_kernel, ring),
        out_shape=[jax.ShapeDtypeStruct((rows, width), BF)] * PARTS,
        in_specs=[hbm, hbm],
        out_specs=[vm] * PARTS,
        scratch_shapes=[
            pltpu.VMEM(occ.shape, BF),
            pltpu.VMEM(slab.shape, BF),
            pltpu.SemaphoreType.DMA,
            pltpu.SemaphoreType.DMA((PARTS,)),
        ],
        compiler_params=pltpu.CompilerParams(vmem_limit_bytes=FIRST_VMEM),
        cost_estimate=pl.CostEstimate(flops=2 * rows * slab.size, bytes_accessed=3 << 20, transcendentals=0),
    )(occ, slab)


def pick_kernel(ring, occ_ref, w_ref):
    rows = occ_ref.shape[1] // ring
    for i in range(ring // 2):
        w_ref[i] = pick_rows(occ_ref[...], rows, ring, ring // 2 - 1 - i)


def pick_rest(occ, ring):
    rows = occ.shape[1] // ring
    return pl.pallas_call(
        functools.partial(pick_kernel, ring),
        out_shape=jax.ShapeDtypeStruct((ring // 2, rows, occ.shape[0]), BF),
        in_specs=[pl.BlockSpec(memory_space=pltpu.VMEM)],
        out_specs=pl.BlockSpec(memory_space=pltpu.VMEM),
        compiler_params=pltpu.CompilerParams(vmem_limit_bytes=VMEM_LIMIT),
        cost_estimate=pl.CostEstimate(flops=2 * (ring // 2) * rows * occ.size, bytes_accessed=2 << 20, transcendentals=0),
    )(occ)


def term_kernel(w_ref, slab_ref, *out_refs):
    cut = slab_ref.shape[0] // PARTS
    for c in range(PARTS):
        out_refs[c][...] = nt(w_ref[0], slab_ref[c * cut : (c + 1) * cut]).astype(BF)


def term(w, i, slab):
    rows, width = w.shape[1], slab.shape[0] // PARTS
    vm = pl.BlockSpec(memory_space=pltpu.VMEM)
    return pl.pallas_call(
        term_kernel,
        grid=(1,),
        out_shape=[jax.ShapeDtypeStruct((rows, width), BF)] * PARTS,
        in_specs=[pl.BlockSpec((1,) + w.shape[1:], lambda g: (i, 0, 0)), vm],
        out_specs=[vm] * PARTS,
        compiler_params=pltpu.CompilerParams(vmem_limit_bytes=VMEM_LIMIT),
        cost_estimate=pl.CostEstimate(flops=2 * rows * slab.size, bytes_accessed=3 << 20, transcendentals=0),
    )(w, slab)


def add(x, y):
    return (x.astype(F32) + y.astype(F32)).astype(BF)


def body(three_index, occ_coef, pao_coef, ao_map, aux_map, ao_list):
    doms, ring = lax.axis_size("dom"), lax.axis_size("ao")
    aux_rows, mu_rows, nu_local = three_index.shape
    blocks = ao_list.shape[0]
    pao_d = pao_coef.shape[2]
    slab = three_index.reshape(aux_rows * mu_rows, nu_local)

    own = first_term(occ_coef, slab, ring)
    w = pick_rest(occ_coef, ring)
    slab, own = lax.optimization_barrier((slab, own))
    other_slab = swap(slab, doms)
    other = None
    half_ring = ring // 2
    for i in range(half_ring):
        own = [add(t, hop(v, doms, ring)) for t, v in zip(term(w, i, slab), own)]
        if i < half_ring - 1:
            if i == 0:
                other = term(w, i, other_slab)
            else:
                other = [add(t, v) for t, v in zip(term(w, i, other_slab), other)]
            other = [hop(v, doms, ring) for v in other]
    halves = [add(v, swap(o, doms)) for v, o in zip(own, other)]

    shells = pao_coef[0].reshape(-1, AOB, pao_d)
    keep = ao_map[0].astype(BF)[ao_list]
    projector = (shells[ao_list] * keep[:, :, None, None]).reshape(blocks, mu_rows, pao_d)
    aux_keep = jnp.repeat(aux_map[0], QB).astype(BF)
    half = jnp.stack([h.reshape(doms, OCC_D, aux_rows // PARTS, mu_rows) for h in halves], axis=2)
    half = half.reshape(doms, OCC_D, aux_rows, mu_rows)
    got = lax.all_to_all(half, "dom", split_axis=0, concat_axis=0, tiled=True)
    got = got.transpose(1, 0, 2, 3).reshape(OCC_D, blocks, QB, mu_rows)
    full = jnp.einsum("kbqm,bma->bqka", got, projector, preferred_element_type=F32)
    full = full.astype(BF).reshape(blocks * QB, OCC_D * pao_d)
    near = lax.ppermute(full, "dom", [(d, (d + 1) % doms) for d in range(doms)])
    fitted = full * aux_keep[:, None]
    pair_self = jnp.einsum("qx,qy->xy", fitted, full, preferred_element_type=F32)
    pair_near = jnp.einsum("qx,qy->xy", fitted, near, preferred_element_type=F32)
    return (pair_self.astype(BF)[None], pair_near.astype(BF)[None])


def solution(mesh):
    owner = P(("dom", "ao"), None, None)
    placed = (
        P("dom", None, "ao"),
        P("ao", None),
        owner,
        P(("dom", "ao"), None),
        P(("dom", "ao"), None),
        P(),
    )
    return jax.shard_map(body, mesh=mesh, in_specs=placed, out_specs=(owner, owner), check_vma=False)
```

time: 127 us -> 103 us (0.81)
  waiting for transfers between devices: 83.2 us -> 50 us
  starting transfers between devices: 12.2 us -> 34.4 us
  between operations: 14.1 us -> 0.99 us
  Pallas kernels: 0 us -> 10.8 us
  local copies, waits for them, and re-layouts: 8.27 us -> 3.19 us
  matrix products: 5.87 us -> 2.3 us
  other arithmetic: 2.58 us -> 1.1 us
    reduce_scatter x1 -> x0, waiting for transfers between devices: 63.4 us -> none  [body(): lax.psum_scatter(term_block.reshape(span_count * dom_count, aux_rows, OCC...]
    ppermute x1 -> x10, waiting for transfers between devices: 6.59 us -> 34.2 us  [the longest x7 27.5 us: hop(): return lax.ppermute(value, ('dom', 'ao'), pairs)]
    ppermute x1 -> x10, starting transfers between devices: 1.92 us -> 23.9 us  [the longest x7 18.2 us: hop(): return lax.ppermute(value, ('dom', 'ao'), pairs)]
    pallas_call x0 -> x9, Pallas kernels: none -> 10.8 us  [the longest x7 5.67 us: term(): pl.pallas_call(term_kernel, grid=(1,), out_shape=[jax.ShapeDtypeStruct((r...]
    dot_general x4 -> x3, matrix products: 5.87 us -> 2.3 us  [the longest x1 1.05 us: body(): jnp.einsum('qx,qy->xy', fitted, near, preferred_element_type=F32)]
    convert_element_type x3 -> x2, local copies, waits for them, and re-layouts: 3.11 us -> 0.24 us  [the longest x1 0.17 us: body(): full = full.astype(BF).reshape(blocks * QB, OCC_D * pao_d)]
    all_to_all x1, waiting for transfers between devices: 13.3 us -> 15.8 us  [body(): got = lax.all_to_all(half, 'dom', split_axis=0, concat_axis=0, tiled=True)]
    mul x1, other arithmetic: 2.54 us -> 0.2 us  [body(): shells[ao_list] * keep[:, :, None, None]]
  transfers between devices with their start and end apart: 3 -> 11, of which waited for: 3 -> 9; matrix products, arithmetic and copies ran while one was open for 5% -> 4% of each run, Pallas kernels for 0% -> 7%
where the time goes in v1:
time: 103 us
  waiting for transfers between devices  50 us (49%)
  starting transfers between devices  34.4 us (33%)
  Pallas kernels  10.8 us (10%)
  local copies, waits for them, and re-layouts  3.19 us (3%)
  matrix products  2.3 us (2%)
  other arithmetic  1.1 us (1%)
    ppermute x7, waiting for transfers between devices, hop(): return lax.ppermute(value, ('dom', 'ao'), pairs)  27.5 us
    ppermute x7, starting transfers between devices, hop(): return lax.ppermute(value, ('dom', 'ao'), pairs)  18.2 us
    all_to_all x1, waiting for transfers between devices, body(): got = lax.all_to_all(half, 'dom', split_axis=0, concat_axis=0, tiled=True)  15.8 us
    all_to_all x1, starting transfers between devices, body(): got = lax.all_to_all(half, 'dom', split_axis=0, concat_axis=0, tiled=True)  10.5 us
    ppermute x1, waiting for transfers between devices, body(): near = lax.ppermute(full, 'dom', [(d, (d + 1) % doms) for d in range(doms)])  6.69 us
    pallas_call x7, Pallas kernels, term(): pl.pallas_call(term_kernel, grid=(1,), out_shape=[jax.ShapeDtypeStruct((r...  5.67 us
    ppermute x2, starting transfers between devices, swap(): return lax.ppermute(value, 'dom', [(d, d ^ 1) for d in range(doms)])  3.83 us
    pallas_call x1, Pallas kernels, first_term(): pl.pallas_call(functools.partial(first_kernel, ring), out_shape=[jax.Shap...  3.68 us
  transfers between devices with their start and end apart: 11, of which 9 were waited for; matrix products, arithmetic and copies ran while one was open for 4% of the time, Pallas kernels for 7%

profile of v1, /device:TPU:16, one launch (start us, length us, event | category | flops | bytes accessed | tf_op | source)
XLA Modules:
  0.0 102.8 jit_solution(10651274498136537617)
XLA Ops:
  0.7 3.7 %shard_map.78 = bf16[128,2048]{1,0:T(8,128)(2,1)} custom-call(bf16[512,1024]{1,0:T(8,128)(2,1)} %occ_hbm.1, bf16[2048,512]{1,0:T(8,128)(2,1)} %bitcast.44), custom_call_target="tpu_custom_call" | custom-call | flops 268435456 | bytes 3145728 | tf_op jit(solution)/shard_map/pallas_call | solution.py:68
  4.4 1.9 %collective-permute-start.4 = (bf16[2048,512]{1,0:T(8,128)(2,1)S(1)}, bf16[2048,512]{1,0:T(8,128)(2,1)S(1)}, u32[]{:S(2)}, u32[]{:S(2)}) collective-permute-start(bf16[2048,512]{1,0:T(8,128)(2,1)S(1)} %bitcast.45), channel_id=1, source_target_pairs={{0,8},{8,0},{16,24},{24,16},{32,40},{40,32},{48,56},{56,48},{64,72... | collective-permute-start | bytes 6291464 | tf_op jit(solution)/shard_map/ppermute | solution.py:30
  6.3 4.3 %collective-permute-start = (bf16[128,2048]{1,0:T(8,128)(2,1)}, bf16[128,2048]{1,0:T(8,128)(2,1)S(1)}, u32[]{:S(2)}, u32[]{:S(2)}) collective-permute-start(bf16[128,2048]{1,0:T(8,128)(2,1)} %shard_map.78), channel_id=1, source_target_pairs={{0,1},{1,2},{2,3},{3,4},{4,5},{5,6},{6,7},{7,0},{8,15},{9,8},{10,9... | collective-permute-start | bytes 1572872 | tf_op jit(solution)/shard_map/ppermute | solution.py:26
  10.6 1.5 %shard_map.77.w_ref = bf16[4,128,512]{2,1,0:T(8,128)(2,1)S(1)} custom-call(bf16[512,1024]{1,0:T(8,128)(2,1)S(1)} %copy-done.2), custom_call_target="tpu_custom_call" | custom-call | flops 536870912 | bytes 2097152 | tf_op jit(solution)/shard_map/pallas_call | solution.py:92
  12.1 0.8 shard_map.85
  12.9 4.3 %collective-permute-start.5 = (bf16[128,2048]{1,0:T(8,128)(2,1)S(1)}, bf16[128,2048]{1,0:T(8,128)(2,1)S(1)}, u32[]{:S(2)}, u32[]{:S(2)}) collective-permute-start(bf16[128,2048]{1,0:T(8,128)(2,1)S(1)} %shard_map.85), channel_id=1, source_target_pairs={{0,1},{1,2},{2,3},{3,4},{4,5},{5,6},{6,7},{7,0},{8,15},{9,8},{10,9... | collective-permute-start | bytes 1572872 | tf_op jit(solution)/shard_map/ppermute | solution.py:26
  17.2 0.8 shard_map.82
  18.0 6.6 %collective-permute-done = bf16[128,2048]{1,0:T(8,128)(2,1)S(1)} collective-permute-done((bf16[128,2048]{1,0:T(8,128)(2,1)}, bf16[128,2048]{1,0:T(8,128)(2,1)S(1)}, u32[]{:S(2)}, u32[]{:S(2)}) %collective-permute-start) | collective-permute-done | bytes 524320 | tf_op jit(solution)/shard_map/ppermute | solution.py:26
  24.7 1.9 %collective-permute-start.1 = (bf16[128,2048]{1,0:T(8,128)(2,1)S(1)}, bf16[128,2048]{1,0:T(8,128)(2,1)S(1)}, u32[]{:S(2)}, u32[]{:S(2)}) collective-permute-start(bf16[128,2048]{1,0:T(8,128)(2,1)S(1)} %add_convert_fusion.6), channel_id=1, source_target_pairs={{0,1},{1,2},{2,3},{3,4},{4,5},{5,6},{6,7},{7,0},{8,15},{9,8},{10,9... | collective-permute-start | bytes 1572872 | tf_op jit(solution)/shard_map/ppermute | solution.py:26
  26.7 0.8 shard_map.84
  27.5 2.7 %collective-permute-done.5 = bf16[128,2048]{1,0:T(8,128)(2,1)S(1)} collective-permute-done((bf16[128,2048]{1,0:T(8,128)(2,1)S(1)}, bf16[128,2048]{1,0:T(8,128)(2,1)S(1)}, u32[]{:S(2)}, u32[]{:S(2)}) %collective-permute-start.5) | collective-permute-done | bytes 524320 | tf_op jit(solution)/shard_map/ppermute | solution.py:26
  30.4 1.9 %collective-permute-start.6 = (bf16[128,2048]{1,0:T(8,128)(2,1)S(1)}, bf16[128,2048]{1,0:T(8,128)(2,1)S(1)}, u32[]{:S(2)}, u32[]{:S(2)}) collective-permute-start(bf16[128,2048]{1,0:T(8,128)(2,1)S(1)} %add_convert_fusion.2), channel_id=1, source_target_pairs={{0,1},{1,2},{2,3},{3,4},{4,5},{5,6},{6,7},{7,0},{8,15},{9,8},{10,9... | collective-permute-start | bytes 1572872 | tf_op jit(solution)/shard_map/ppermute | solution.py:26
  32.3 0.8 shard_map.81
  33.1 3.9 %collective-permute-done.1 = bf16[128,2048]{1,0:T(8,128)(2,1)S(1)} collective-permute-done((bf16[128,2048]{1,0:T(8,128)(2,1)S(1)}, bf16[128,2048]{1,0:T(8,128)(2,1)S(1)}, u32[]{:S(2)}, u32[]{:S(2)}) %collective-permute-start.1) | collective-permute-done | bytes 524320 | tf_op jit(solution)/shard_map/ppermute | solution.py:26
  37.1 1.9 %collective-permute-start.2 = (bf16[128,2048]{1,0:T(8,128)(2,1)S(1)}, bf16[128,2048]{1,0:T(8,128)(2,1)S(1)}, u32[]{:S(2)}, u32[]{:S(2)}) collective-permute-start(bf16[128,2048]{1,0:T(8,128)(2,1)S(1)} %add_convert_fusion.5), channel_id=1, source_target_pairs={{0,1},{1,2},{2,3},{3,4},{4,5},{5,6},{6,7},{7,0},{8,15},{9,8},{10,9... | collective-permute-start | bytes 1572872 | tf_op jit(solution)/shard_map/ppermute | solution.py:26
  39.1 0.8 shard_map.83
  39.9 2.7 %collective-permute-done.6 = bf16[128,2048]{1,0:T(8,128)(2,1)S(1)} collective-permute-done((bf16[128,2048]{1,0:T(8,128)(2,1)S(1)}, bf16[128,2048]{1,0:T(8,128)(2,1)S(1)}, u32[]{:S(2)}, u32[]{:S(2)}) %collective-permute-start.6) | collective-permute-done | bytes 524320 | tf_op jit(solution)/shard_map/ppermute | solution.py:26
  42.8 1.9 %collective-permute-start.7 = (bf16[128,2048]{1,0:T(8,128)(2,1)S(1)}, bf16[128,2048]{1,0:T(8,128)(2,1)S(1)}, u32[]{:S(2)}, u32[]{:S(2)}) collective-permute-start(bf16[128,2048]{1,0:T(8,128)(2,1)S(1)} %add_convert_fusion.1), channel_id=1, source_target_pairs={{0,1},{1,2},{2,3},{3,4},{4,5},{5,6},{6,7},{7,0},{8,15},{9,8},{10,9... | collective-permute-start | bytes 1572872 | tf_op jit(solution)/shard_map/ppermute | solution.py:26
  44.7 0.8 shard_map.80
  45.5 3.9 %collective-permute-done.2 = bf16[128,2048]{1,0:T(8,128)(2,1)S(1)} collective-permute-done((bf16[128,2048]{1,0:T(8,128)(2,1)S(1)}, bf16[128,2048]{1,0:T(8,128)(2,1)S(1)}, u32[]{:S(2)}, u32[]{:S(2)}) %collective-permute-start.2) | collective-permute-done | bytes 524320 | tf_op jit(solution)/shard_map/ppermute | solution.py:26
  49.6 1.9 %collective-permute-start.3 = (bf16[128,2048]{1,0:T(8,128)(2,1)S(1)}, bf16[128,2048]{1,0:T(8,128)(2,1)S(1)}, u32[]{:S(2)}, u32[]{:S(2)}) collective-permute-start(bf16[128,2048]{1,0:T(8,128)(2,1)S(1)} %add_convert_fusion.4), channel_id=1, source_target_pairs={{0,1},{1,2},{2,3},{3,4},{4,5},{5,6},{6,7},{7,0},{8,15},{9,8},{10,9... | collective-permute-start | bytes 1572872 | tf_op jit(solution)/shard_map/ppermute | solution.py:26
  51.5 3.6 %collective-permute-done.7 = bf16[128,2048]{1,0:T(8,128)(2,1)S(1)} collective-permute-done((bf16[128,2048]{1,0:T(8,128)(2,1)S(1)}, bf16[128,2048]{1,0:T(8,128)(2,1)S(1)}, u32[]{:S(2)}, u32[]{:S(2)}) %collective-permute-start.7) | collective-permute-done | bytes 524320 | tf_op jit(solution)/shard_map/ppermute | solution.py:26
  55.1 1.9 %collective-permute-start.8 = (bf16[128,2048]{1,0:T(8,128)(2,1)S(1)}, bf16[128,2048]{1,0:T(8,128)(2,1)S(1)}, u32[]{:S(2)}, u32[]{:S(2)}) collective-permute-start(bf16[128,2048]{1,0:T(8,128)(2,1)S(1)} %collective-permute-done.7), channel_id=1, source_target_pairs={{0,8},{8,0},{16,24},{24,16},{32,40},{40,32},{48,56},{56,48},{64,72... | collective-permute-start | bytes 1572872 | tf_op jit(solution)/shard_map/ppermute | solution.py:30
  57.0 0.8 shard_map.79
  57.8 4.0 %collective-permute-done.3 = bf16[128,2048]{1,0:T(8,128)(2,1)S(1)} collective-permute-done((bf16[128,2048]{1,0:T(8,128)(2,1)S(1)}, bf16[128,2048]{1,0:T(8,128)(2,1)S(1)}, u32[]{:S(2)}, u32[]{:S(2)}) %collective-permute-start.3) | collective-permute-done | bytes 524320 | tf_op jit(solution)/shard_map/ppermute | solution.py:26
  62.1 0.9 copy.21
  63.0 10.5 %all-to-all-start = ((bf16[64,2,8,256]{3,2,1,0:T(8,128)(2,1)}), bf16[64,2,8,256]{3,2,1,0:T(8,128)(2,1)S(1)}, u32[]{:S(2)}, u32[]{:S(2)}) async-start(bf16[64,2,8,256]{3,2,1,0:T(8,128)(2,1)} %bitcast.16), calls=%async_computation | async-start | bytes 1048576 | tf_op jit(solution)/shard_map/all_to_all | solution.py:155
  75.5 15.8 %all-to-all-done = bf16[64,2,8,256]{3,2,1,0:T(8,128)(2,1)S(1)} async-done(((bf16[64,2,8,256]{3,2,1,0:T(8,128)(2,1)}), bf16[64,2,8,256]{3,2,1,0:T(8,128)(2,1)S(1)}, u32[]{:S(2)}, u32[]{:S(2)}) %all-to-all-start) | async-done | bytes 524320 | tf_op jit(solution)/shard_map/all_to_all | solution.py:155
  91.9 1.9 %collective-permute-start.9 = (bf16[512,256]{1,0:T(8,128)(2,1)S(1)}, bf16[512,256]{1,0:T(8,128)(2,1)S(1)}, u32[]{:S(2)}, u32[]{:S(2)}) collective-permute-start(bf16[512,256]{1,0:T(8,128)(2,1)S(1)} %bitcast.56), channel_id=1, source_target_pairs={{0,8},{8,16},{16,24},{24,32},{32,40},{40,48},{48,56},{56,64},{64,7... | collective-permute-start | bytes 786440 | tf_op jit(solution)/shard_map/ppermute | solution.py:159
  94.1 0.9 fusion.1
  95.0 6.7 %collective-permute-done.9 = bf16[512,256]{1,0:T(8,128)(2,1)S(1)} collective-permute-done((bf16[512,256]{1,0:T(8,128)(2,1)S(1)}, bf16[512,256]{1,0:T(8,128)(2,1)S(1)}, u32[]{:S(2)}, u32[]{:S(2)}) %collective-permute-start.9) | collective-permute-done | bytes 262176 | tf_op jit(solution)/shard_map/ppermute | solution.py:159
  101.7 1.1 %fusion.2 = bf16[1,256,256]{2,1,0:T(8,128)(2,1)} fusion(bf16[512,256]{1,0:T(8,128)(2,1)S(1)} %collective-permute-done.9, bf16[512]{0:T(512)(128)(2,1)S(1)} %broadcast_bitcast_fusion, bf16[64,8,2,128]{3,2,1,0:T(2,128)(2,1)S(1)} %bitcast.54), kind=kOutput, calls=%fused_computation.7 | convolution fusion | flops 67305472 | bytes 656384 | tf_op jit(solution)/shard_map/qx,qy->xy/dot_general | solution.py:162
  (37 shorter events, 3.7 us)
Async XLA Ops:
  0.6 73.0 %copy-start = (bf16[1,4096,128]{2,1,0:T(8,128)(2,1)S(1)}, bf16[1,4096,128]{2,1,0:T(8,128)(2,1)}, u32[]{:S(2)}) copy-start(bf16[1,4096,128]{2,1,0:T(8,128)(2,1)} %param.8) | copy-start | bytes 3145732
  0.6 3.7 %copy-start.1 = (bf16[8,256,512]{2,1,0:T(8,128)(2,1)S(1)}, bf16[8,256,512]{2,1,0:T(8,128)(2,1)}, u32[]{:S(2)}) copy-start(bf16[8,256,512]{2,1,0:T(8,128)(2,1)} %param.6) | copy-start | bytes 6291460
  0.7 9.9 %copy-start.2 = (bf16[512,1024]{1,0:T(8,128)(2,1)S(1)}, bf16[512,1024]{1,0:T(8,128)(2,1)}, u32[]{:S(2)}) copy-start(bf16[512,1024]{1,0:T(8,128)(2,1)} %occ_hbm.1) | copy-start | bytes 3145732
  4.4 7.7 %collective-permute-start.4 = (bf16[2048,512]{1,0:T(8,128)(2,1)S(1)}, bf16[2048,512]{1,0:T(8,128)(2,1)S(1)}, u32[]{:S(2)}, u32[]{:S(2)}) collective-permute-start(bf16[2048,512]{1,0:T(8,128)(2,1)S(1)} %bitcast.45), channel_id=1, source_target_pairs={{0,8},{8,0},{16,24},{24,16},{32,40},{40,32},{48,56},{56,48},{64,72... | collective-permute-start | bytes 6291464 | tf_op jit(solution)/shard_map/ppermute | solution.py:30
  6.3 18.3 %collective-permute-start = (bf16[128,2048]{1,0:T(8,128)(2,1)}, bf16[128,2048]{1,0:T(8,128)(2,1)S(1)}, u32[]{:S(2)}, u32[]{:S(2)}) collective-permute-start(bf16[128,2048]{1,0:T(8,128)(2,1)} %shard_map.78), channel_id=1, source_target_pairs={{0,1},{1,2},{2,3},{3,4},{4,5},{5,6},{6,7},{7,0},{8,15},{9,8},{10,9... | collective-permute-start | bytes 1572872 | tf_op jit(solution)/shard_map/ppermute | solution.py:26
  12.9 17.3 %collective-permute-start.5 = (bf16[128,2048]{1,0:T(8,128)(2,1)S(1)}, bf16[128,2048]{1,0:T(8,128)(2,1)S(1)}, u32[]{:S(2)}, u32[]{:S(2)}) collective-permute-start(bf16[128,2048]{1,0:T(8,128)(2,1)S(1)} %shard_map.85), channel_id=1, source_target_pairs={{0,1},{1,2},{2,3},{3,4},{4,5},{5,6},{6,7},{7,0},{8,15},{9,8},{10,9... | collective-permute-start | bytes 1572872 | tf_op jit(solution)/shard_map/ppermute | solution.py:26
  24.7 12.3 %collective-permute-start.1 = (bf16[128,2048]{1,0:T(8,128)(2,1)S(1)}, bf16[128,2048]{1,0:T(8,128)(2,1)S(1)}, u32[]{:S(2)}, u32[]{:S(2)}) collective-permute-start(bf16[128,2048]{1,0:T(8,128)(2,1)S(1)} %add_convert_fusion.6), channel_id=1, source_target_pairs={{0,1},{1,2},{2,3},{3,4},{4,5},{5,6},{6,7},{7,0},{8,15},{9,8},{10,9... | collective-permute-start | bytes 1572872 | tf_op jit(solution)/shard_map/ppermute | solution.py:26
  30.4 12.3 %collective-permute-start.6 = (bf16[128,2048]{1,0:T(8,128)(2,1)S(1)}, bf16[128,2048]{1,0:T(8,128)(2,1)S(1)}, u32[]{:S(2)}, u32[]{:S(2)}) collective-permute-start(bf16[128,2048]{1,0:T(8,128)(2,1)S(1)} %add_convert_fusion.2), channel_id=1, source_target_pairs={{0,1},{1,2},{2,3},{3,4},{4,5},{5,6},{6,7},{7,0},{8,15},{9,8},{10,9... | collective-permute-start | bytes 1572872 | tf_op jit(solution)/shard_map/ppermute | solution.py:26
  37.1 12.3 %collective-permute-start.2 = (bf16[128,2048]{1,0:T(8,128)(2,1)S(1)}, bf16[128,2048]{1,0:T(8,128)(2,1)S(1)}, u32[]{:S(2)}, u32[]{:S(2)}) collective-permute-start(bf16[128,2048]{1,0:T(8,128)(2,1)S(1)} %add_convert_fusion.5), channel_id=1, source_target_pairs={{0,1},{1,2},{2,3},{3,4},{4,5},{5,6},{6,7},{7,0},{8,15},{9,8},{10,9... | collective-permute-start | bytes 1572872 | tf_op jit(solution)/shard_map/ppermute | solution.py:26
  42.8 12.3 %collective-permute-start.7 = (bf16[128,2048]{1,0:T(8,128)(2,1)S(1)}, bf16[128,2048]{1,0:T(8,128)(2,1)S(1)}, u32[]{:S(2)}, u32[]{:S(2)}) collective-permute-start(bf16[128,2048]{1,0:T(8,128)(2,1)S(1)} %add_convert_fusion.1), channel_id=1, source_target_pairs={{0,1},{1,2},{2,3},{3,4},{4,5},{5,6},{6,7},{7,0},{8,15},{9,8},{10,9... | collective-permute-start | bytes 1572872 | tf_op jit(solution)/shard_map/ppermute | solution.py:26
  49.6 12.3 %collective-permute-start.3 = (bf16[128,2048]{1,0:T(8,128)(2,1)S(1)}, bf16[128,2048]{1,0:T(8,128)(2,1)S(1)}, u32[]{:S(2)}, u32[]{:S(2)}) collective-permute-start(bf16[128,2048]{1,0:T(8,128)(2,1)S(1)} %add_convert_fusion.4), channel_id=1, source_target_pairs={{0,1},{1,2},{2,3},{3,4},{4,5},{5,6},{6,7},{7,0},{8,15},{9,8},{10,9... | collective-permute-start | bytes 1572872 | tf_op jit(solution)/shard_map/ppermute | solution.py:26
  55.1 6.8 %collective-permute-start.8 = (bf16[128,2048]{1,0:T(8,128)(2,1)S(1)}, bf16[128,2048]{1,0:T(8,128)(2,1)S(1)}, u32[]{:S(2)}, u32[]{:S(2)}) collective-permute-start(bf16[128,2048]{1,0:T(8,128)(2,1)S(1)} %collective-permute-done.7), channel_id=1, source_target_pairs={{0,8},{8,0},{16,24},{24,16},{32,40},{40,32},{48,56},{56,48},{64,72... | collective-permute-start | bytes 1572872 | tf_op jit(solution)/shard_map/ppermute | solution.py:30
  57.8 15.7 %copy-start.3 = (s32[4,16]{1,0:T(4,128)S(1)}, s32[4,16]{1,0:T(4,128)}, u32[]{:S(2)}) copy-start(s32[4,16]{1,0:T(4,128)} %param.11) | copy-start | bytes 772
  57.8 16.4 %copy-start.4 = (s32[1,256]{1,0:T(1,128)S(1)}, s32[1,256]{1,0:T(1,128)}, u32[]{:S(2)}) copy-start(s32[1,256]{1,0:T(1,128)} %param.9) | copy-start | bytes 3076
  62.1 13.2 %copy-start.5 = (s32[1,4]{1,0:T(1,128)S(1)}, s32[1,4]{1,0:T(1,128)}, u32[]{:S(2)}) copy-start(s32[1,4]{1,0:T(1,128)} %param.10) | copy-start | bytes 52
  63.0 28.3 %all-to-all-start = ((bf16[64,2,8,256]{3,2,1,0:T(8,128)(2,1)}), bf16[64,2,8,256]{3,2,1,0:T(8,128)(2,1)S(1)}, u32[]{:S(2)}, u32[]{:S(2)}) async-start(bf16[64,2,8,256]{3,2,1,0:T(8,128)(2,1)} %bitcast.16), calls=%async_computation | async-start | bytes 1048576 | tf_op jit(solution)/shard_map/all_to_all | solution.py:155
  91.9 9.8 %collective-permute-start.9 = (bf16[512,256]{1,0:T(8,128)(2,1)S(1)}, bf16[512,256]{1,0:T(8,128)(2,1)S(1)}, u32[]{:S(2)}, u32[]{:S(2)}) collective-permute-start(bf16[512,256]{1,0:T(8,128)(2,1)S(1)} %bitcast.56), channel_id=1, source_target_pairs={{0,8},{8,16},{16,24},{24,32},{32,40},{40,48},{48,56},{56,64},{64,7... | collective-permute-start | bytes 786440 | tf_op jit(solution)/shard_map/ppermute | solution.py:159

commit v2 on v1

--- a/solution.py
+++ b/solution.py
@@ -10,6 +10,7 @@
 QB = 128
 AOB = 16
 OCC_D = 2
+vm = pl.BlockSpec(memory_space=pltpu.VMEM)
 BF = jnp.bfloat16
 F32 = jnp.float32
 PARTS = 1
@@ -123,6 +124,71 @@
     return (x.astype(F32) + y.astype(F32)).astype(BF)
 
 
+def cost(flops, size):
+    return pl.CostEstimate(flops=flops, bytes_accessed=size, transcendentals=0)
+
+
+def full_kernel(got_ref, projector_ref, full_ref):
+    doms, _, aux_rows, mu_rows = got_ref.shape
+    blocks, _, pao_d = projector_ref.shape
+    per = doms // blocks
+    for b in range(blocks):
+        part = got_ref[b * per : (b + 1) * per].astype(F32).reshape(per * OCC_D * aux_rows, mu_rows).astype(BF)
+        t = jnp.dot(part, projector_ref[b], preferred_element_type=F32).reshape(per, OCC_D, aux_rows, pao_d)
+        for k in range(OCC_D):
+            rows = slice(b * per * aux_rows, (b + 1) * per * aux_rows)
+            full_ref[rows, k * pao_d : (k + 1) * pao_d] = t[:, k].reshape(per * aux_rows, pao_d).astype(BF)
+
+
+def full_of(got, projector):
+    doms, _, aux_rows, _ = got.shape
+    return pl.pallas_call(
+        full_kernel,
+        out_shape=jax.ShapeDtypeStruct((doms * aux_rows, OCC_D * projector.shape[2]), BF),
+        in_specs=[vm, vm],
+        out_specs=vm,
+        compiler_params=pltpu.CompilerParams(vmem_limit_bytes=VMEM_LIMIT),
+        cost_estimate=cost(2 * got.size * projector.shape[2], 1 << 20),
+    )(got, projector)
+
+
+def self_kernel(full_ref, keep_ref, out_ref, turned_ref):
+    per = full_ref.shape[0] // keep_ref.shape[1]
+    for b in range(keep_ref.shape[1]):
+        rows = slice(b * per, (b + 1) * per)
+        kept = full_ref[rows].astype(F32) * keep_ref[0, b].astype(F32)
+        turned_ref[:, rows] = kept.T.astype(BF)
+    out_ref[0] = jnp.dot(turned_ref[...], full_ref[...], preferred_element_type=F32).astype(BF)
+
+
+def self_pair(full, aux_map):
+    rows, width = full.shape
+    return pl.pallas_call(
+        self_kernel,
+        out_shape=[jax.ShapeDtypeStruct((1, width, width), BF), jax.ShapeDtypeStruct((width, rows), BF)],
+        in_specs=[vm, pl.BlockSpec(memory_space=pltpu.SMEM)],
+        out_specs=[vm, vm],
+        compiler_params=pltpu.CompilerParams(vmem_limit_bytes=VMEM_LIMIT),
+        cost_estimate=cost(2 * rows * width * width, 1 << 20),
+    )(full, aux_map)
+
+
+def near_kernel(turned_ref, near_ref, out_ref):
+    out_ref[0] = jnp.dot(turned_ref[...], near_ref[...], preferred_element_type=F32).astype(BF)
+
+
+def near_pair(turned, near):
+    rows, width = near.shape
+    return pl.pallas_call(
+        near_kernel,
+        out_shape=jax.ShapeDtypeStruct((1, width, width), BF),
+        in_specs=[vm, vm],
+        out_specs=vm,
+        compiler_params=pltpu.CompilerParams(vmem_limit_bytes=VMEM_LIMIT),
+        cost_estimate=cost(2 * rows * width * width, 1 << 20),
+    )(turned, near)
+
+
 def body(three_index, occ_coef, pao_coef, ao_map, aux_map, ao_list):
     doms, ring = lax.axis_size("dom"), lax.axis_size("ao")
     aux_rows, mu_rows, nu_local = three_index.shape
@@ -149,18 +215,14 @@
     shells = pao_coef[0].reshape(-1, AOB, pao_d)
     keep = ao_map[0].astype(BF)[ao_list]
     projector = (shells[ao_list] * keep[:, :, None, None]).reshape(blocks, mu_rows, pao_d)
-    aux_keep = jnp.repeat(aux_map[0], QB).astype(BF)
     half = jnp.stack([h.reshape(doms, OCC_D, aux_rows // PARTS, mu_rows) for h in halves], axis=2)
     half = half.reshape(doms, OCC_D, aux_rows, mu_rows)
     got = lax.all_to_all(half, "dom", split_axis=0, concat_axis=0, tiled=True)
-    got = got.transpose(1, 0, 2, 3).reshape(OCC_D, blocks, QB, mu_rows)
-    full = jnp.einsum("kbqm,bma->bqka", got, projector, preferred_element_type=F32)
-    full = full.astype(BF).reshape(blocks * QB, OCC_D * pao_d)
+    full = full_of(got, projector)
     near = lax.ppermute(full, "dom", [(d, (d + 1) % doms) for d in range(doms)])
-    fitted = full * aux_keep[:, None]
-    pair_self = jnp.einsum("qx,qy->xy", fitted, full, preferred_element_type=F32)
-    pair_near = jnp.einsum("qx,qy->xy", fitted, near, preferred_element_type=F32)
-    return (pair_self.astype(BF)[None], pair_near.astype(BF)[None])
+    pair_self, turned = self_pair(full, aux_map)
+    pair_near = near_pair(turned, near)
+    return (pair_self, pair_near)
 
 
 def solution(mesh):

time: 103 us -> 103 us (level)
  Pallas kernels: 10.8 us -> 13.5 us
  matrix products: 2.3 us -> 0 us
    pallas_call x0 -> x3, Pallas kernels: none -> 2.67 us  [the longest x1 1.5 us: self_pair(): pl.pallas_call(self_kernel, out_shape=[jax.ShapeDtypeStruct((1, width, wi...]
    dot_general x3 -> x0, matrix products: 2.3 us -> none  [the longest x1 1.05 us: body(): jnp.einsum('qx,qy->xy', fitted, near, preferred_element_type=F32)]
  transfers between devices with their start and end apart: 11 -> 11, of which waited for: 9 -> 9; matrix products, arithmetic and copies ran while one was open for 4% -> 3% of each run, Pallas kernels for 7% -> 8%
where the time goes in v2:
time: 103 us; the launch traced here: 102 us
  waiting for transfers between devices  49.7 us (48%)
  starting transfers between devices  34.5 us (33%)
  Pallas kernels  13.5 us (13%)
  local copies, waits for them, and re-layouts  2.69 us (3%)
  other arithmetic  1.11 us (1%)
    ppermute x7, waiting for transfers between devices, hop(): return lax.ppermute(value, ('dom', 'ao'), pairs)  27.5 us
    ppermute x7, starting transfers between devices, hop(): return lax.ppermute(value, ('dom', 'ao'), pairs)  18.2 us
    all_to_all x1, waiting for transfers between devices, body(): got = lax.all_to_all(half, 'dom', split_axis=0, concat_axis=0, tiled=True)  15.8 us
    all_to_all x1, starting transfers between devices, body(): got = lax.all_to_all(half, 'dom', split_axis=0, concat_axis=0, tiled=True)  10.6 us
    ppermute x1, waiting for transfers between devices, body(): near = lax.ppermute(full, 'dom', [(d, (d + 1) % doms) for d in range(doms)])  6.36 us
    pallas_call x7, Pallas kernels, term(): pl.pallas_call(term_kernel, grid=(1,), out_shape=[jax.ShapeDtypeStruct((r...  5.67 us
    ppermute x2, starting transfers between devices, swap(): return lax.ppermute(value, 'dom', [(d, d ^ 1) for d in range(doms)])  3.83 us
    pallas_call x1, Pallas kernels, first_term(): pl.pallas_call(functools.partial(first_kernel, ring), out_shape=[jax.Shap...  3.68 us
  transfers between devices with their start and end apart: 11, of which 9 were waited for; matrix products, arithmetic and copies ran while one was open for 3% of the time, Pallas kernels for 8%

profile of v2, /device:TPU:16, one launch (start us, length us, event | category | flops | bytes accessed | tf_op | source)
XLA Modules:
  0.0 102.4 jit_solution(11614254805341667298)
XLA Ops:
  0.7 3.7 %shard_map.78 = bf16[128,2048]{1,0:T(8,128)(2,1)} custom-call(bf16[512,1024]{1,0:T(8,128)(2,1)} %occ_hbm.1, bf16[2048,512]{1,0:T(8,128)(2,1)} %bitcast.9), custom_call_target="tpu_custom_call" | custom-call | flops 268435456 | bytes 3145728 | tf_op jit(solution)/shard_map/pallas_call | solution.py:69
  4.4 1.9 %collective-permute-start.4 = (bf16[2048,512]{1,0:T(8,128)(2,1)S(1)}, bf16[2048,512]{1,0:T(8,128)(2,1)S(1)}, u32[]{:S(2)}, u32[]{:S(2)}) collective-permute-start(bf16[2048,512]{1,0:T(8,128)(2,1)S(1)} %bitcast.10), channel_id=1, source_target_pairs={{0,8},{8,0},{16,24},{24,16},{32,40},{40,32},{48,56},{56,48},{64,72... | collective-permute-start | bytes 6291464 | tf_op jit(solution)/shard_map/ppermute | solution.py:31
  6.3 4.3 %collective-permute-start = (bf16[128,2048]{1,0:T(8,128)(2,1)}, bf16[128,2048]{1,0:T(8,128)(2,1)S(1)}, u32[]{:S(2)}, u32[]{:S(2)}) collective-permute-start(bf16[128,2048]{1,0:T(8,128)(2,1)} %shard_map.78), channel_id=1, source_target_pairs={{0,1},{1,2},{2,3},{3,4},{4,5},{5,6},{6,7},{7,0},{8,15},{9,8},{10,9... | collective-permute-start | bytes 1572872 | tf_op jit(solution)/shard_map/ppermute | solution.py:27
  10.6 1.5 %shard_map.77.w_ref = bf16[4,128,512]{2,1,0:T(8,128)(2,1)S(1)} custom-call(bf16[512,1024]{1,0:T(8,128)(2,1)S(1)} %copy-done.2), custom_call_target="tpu_custom_call" | custom-call | flops 536870912 | bytes 2097152 | tf_op jit(solution)/shard_map/pallas_call | solution.py:93
  12.1 0.8 shard_map.85
  12.9 4.3 %collective-permute-start.5 = (bf16[128,2048]{1,0:T(8,128)(2,1)S(1)}, bf16[128,2048]{1,0:T(8,128)(2,1)S(1)}, u32[]{:S(2)}, u32[]{:S(2)}) collective-permute-start(bf16[128,2048]{1,0:T(8,128)(2,1)S(1)} %shard_map.85), channel_id=1, source_target_pairs={{0,1},{1,2},{2,3},{3,4},{4,5},{5,6},{6,7},{7,0},{8,15},{9,8},{10,9... | collective-permute-start | bytes 1572872 | tf_op jit(solution)/shard_map/ppermute | solution.py:27
  17.2 0.8 shard_map.82
  18.0 6.6 %collective-permute-done = bf16[128,2048]{1,0:T(8,128)(2,1)S(1)} collective-permute-done((bf16[128,2048]{1,0:T(8,128)(2,1)}, bf16[128,2048]{1,0:T(8,128)(2,1)S(1)}, u32[]{:S(2)}, u32[]{:S(2)}) %collective-permute-start) | collective-permute-done | bytes 524320 | tf_op jit(solution)/shard_map/ppermute | solution.py:27
  24.7 1.9 %collective-permute-start.1 = (bf16[128,2048]{1,0:T(8,128)(2,1)S(1)}, bf16[128,2048]{1,0:T(8,128)(2,1)S(1)}, u32[]{:S(2)}, u32[]{:S(2)}) collective-permute-start(bf16[128,2048]{1,0:T(8,128)(2,1)S(1)} %add_convert_fusion.6), channel_id=1, source_target_pairs={{0,1},{1,2},{2,3},{3,4},{4,5},{5,6},{6,7},{7,0},{8,15},{9,8},{10,9... | collective-permute-start | bytes 1572872 | tf_op jit(solution)/shard_map/ppermute | solution.py:27
  26.7 0.8 shard_map.84
  27.5 2.7 %collective-permute-done.5 = bf16[128,2048]{1,0:T(8,128)(2,1)S(1)} collective-permute-done((bf16[128,2048]{1,0:T(8,128)(2,1)S(1)}, bf16[128,2048]{1,0:T(8,128)(2,1)S(1)}, u32[]{:S(2)}, u32[]{:S(2)}) %collective-permute-start.5) | collective-permute-done | bytes 524320 | tf_op jit(solution)/shard_map/ppermute | solution.py:27
  30.4 1.9 %collective-permute-start.6 = (bf16[128,2048]{1,0:T(8,128)(2,1)S(1)}, bf16[128,2048]{1,0:T(8,128)(2,1)S(1)}, u32[]{:S(2)}, u32[]{:S(2)}) collective-permute-start(bf16[128,2048]{1,0:T(8,128)(2,1)S(1)} %add_convert_fusion.2), channel_id=1, source_target_pairs={{0,1},{1,2},{2,3},{3,4},{4,5},{5,6},{6,7},{7,0},{8,15},{9,8},{10,9... | collective-permute-start | bytes 1572872 | tf_op jit(solution)/shard_map/ppermute | solution.py:27
  32.3 0.8 shard_map.81
  33.1 3.9 %collective-permute-done.1 = bf16[128,2048]{1,0:T(8,128)(2,1)S(1)} collective-permute-done((bf16[128,2048]{1,0:T(8,128)(2,1)S(1)}, bf16[128,2048]{1,0:T(8,128)(2,1)S(1)}, u32[]{:S(2)}, u32[]{:S(2)}) %collective-permute-start.1) | collective-permute-done | bytes 524320 | tf_op jit(solution)/shard_map/ppermute | solution.py:27
  37.1 1.9 %collective-permute-start.2 = (bf16[128,2048]{1,0:T(8,128)(2,1)S(1)}, bf16[128,2048]{1,0:T(8,128)(2,1)S(1)}, u32[]{:S(2)}, u32[]{:S(2)}) collective-permute-start(bf16[128,2048]{1,0:T(8,128)(2,1)S(1)} %add_convert_fusion.5), channel_id=1, source_target_pairs={{0,1},{1,2},{2,3},{3,4},{4,5},{5,6},{6,7},{7,0},{8,15},{9,8},{10,9... | collective-permute-start | bytes 1572872 | tf_op jit(solution)/shard_map/ppermute | solution.py:27
  39.1 0.8 shard_map.83
  39.9 2.7 %collective-permute-done.6 = bf16[128,2048]{1,0:T(8,128)(2,1)S(1)} collective-permute-done((bf16[128,2048]{1,0:T(8,128)(2,1)S(1)}, bf16[128,2048]{1,0:T(8,128)(2,1)S(1)}, u32[]{:S(2)}, u32[]{:S(2)}) %collective-permute-start.6) | collective-permute-done | bytes 524320 | tf_op jit(solution)/shard_map/ppermute | solution.py:27
  42.8 1.9 %collective-permute-start.7 = (bf16[128,2048]{1,0:T(8,128)(2,1)S(1)}, bf16[128,2048]{1,0:T(8,128)(2,1)S(1)}, u32[]{:S(2)}, u32[]{:S(2)}) collective-permute-start(bf16[128,2048]{1,0:T(8,128)(2,1)S(1)} %add_convert_fusion.1), channel_id=1, source_target_pairs={{0,1},{1,2},{2,3},{3,4},{4,5},{5,6},{6,7},{7,0},{8,15},{9,8},{10,9... | collective-permute-start | bytes 1572872 | tf_op jit(solution)/shard_map/ppermute | solution.py:27
  44.7 0.8 shard_map.80
  45.5 3.9 %collective-permute-done.2 = bf16[128,2048]{1,0:T(8,128)(2,1)S(1)} collective-permute-done((bf16[128,2048]{1,0:T(8,128)(2,1)S(1)}, bf16[128,2048]{1,0:T(8,128)(2,1)S(1)}, u32[]{:S(2)}, u32[]{:S(2)}) %collective-permute-start.2) | collective-permute-done | bytes 524320 | tf_op jit(solution)/shard_map/ppermute | solution.py:27
  49.6 1.9 %collective-permute-start.3 = (bf16[128,2048]{1,0:T(8,128)(2,1)S(1)}, bf16[128,2048]{1,0:T(8,128)(2,1)S(1)}, u32[]{:S(2)}, u32[]{:S(2)}) collective-permute-start(bf16[128,2048]{1,0:T(8,128)(2,1)S(1)} %add_convert_fusion.4), channel_id=1, source_target_pairs={{0,1},{1,2},{2,3},{3,4},{4,5},{5,6},{6,7},{7,0},{8,15},{9,8},{10,9... | collective-permute-start | bytes 1572872 | tf_op jit(solution)/shard_map/ppermute | solution.py:27
  51.5 3.6 %collective-permute-done.7 = bf16[128,2048]{1,0:T(8,128)(2,1)S(1)} collective-permute-done((bf16[128,2048]{1,0:T(8,128)(2,1)S(1)}, bf16[128,2048]{1,0:T(8,128)(2,1)S(1)}, u32[]{:S(2)}, u32[]{:S(2)}) %collective-permute-start.7) | collective-permute-done | bytes 524320 | tf_op jit(solution)/shard_map/ppermute | solution.py:27
  55.1 1.9 %collective-permute-start.8 = (bf16[128,2048]{1,0:T(8,128)(2,1)S(1)}, bf16[128,2048]{1,0:T(8,128)(2,1)S(1)}, u32[]{:S(2)}, u32[]{:S(2)}) collective-permute-start(bf16[128,2048]{1,0:T(8,128)(2,1)S(1)} %collective-permute-done.7), channel_id=1, source_target_pairs={{0,8},{8,0},{16,24},{24,16},{32,40},{40,32},{48,56},{56,48},{64,72... | collective-permute-start | bytes 1572872 | tf_op jit(solution)/shard_map/ppermute | solution.py:31
  57.0 0.8 shard_map.79
  57.8 4.0 %collective-permute-done.3 = bf16[128,2048]{1,0:T(8,128)(2,1)S(1)} collective-permute-done((bf16[128,2048]{1,0:T(8,128)(2,1)S(1)}, bf16[128,2048]{1,0:T(8,128)(2,1)S(1)}, u32[]{:S(2)}, u32[]{:S(2)}) %collective-permute-start.3) | collective-permute-done | bytes 524320 | tf_op jit(solution)/shard_map/ppermute | solution.py:27
  62.1 0.9 copy.8
  63.0 10.6 %all-to-all-start = ((bf16[64,2,8,256]{3,2,1,0:T(8,128)(2,1)}), bf16[64,2,8,256]{3,2,1,0:T(8,128)(2,1)S(1)}, u32[]{:S(2)}, u32[]{:S(2)}) async-start(bf16[64,2,8,256]{3,2,1,0:T(8,128)(2,1)} %bitcast.5), calls=%async_computation | async-start | bytes 1048576 | tf_op jit(solution)/shard_map/all_to_all | solution.py:220
  75.7 15.8 %all-to-all-done.got_ref = bf16[64,2,8,256]{3,2,1,0:T(8,128)(2,1)S(1)} async-done(((bf16[64,2,8,256]{3,2,1,0:T(8,128)(2,1)}), bf16[64,2,8,256]{3,2,1,0:T(8,128)(2,1)S(1)}, u32[]{:S(2)}, u32[]{:S(2)}) %all-to-all-start) | async-done | bytes 524320 | tf_op jit(solution)/shard_map/all_to_all | solution.py:220
  91.7 1.9 %collective-permute-start.9 = (bf16[512,256]{1,0:T(8,128)(2,1)S(1)}, bf16[512,256]{1,0:T(8,128)(2,1)S(1)}, u32[]{:S(2)}, u32[]{:S(2)}) collective-permute-start(bf16[512,256]{1,0:T(8,128)(2,1)S(1)} %shard_map.86.full_ref), channel_id=1, source_target_pairs={{0,8},{8,16},{16,24},{24,32},{32,40},{40,48},{48,56},{56,64},{64,7... | collective-permute-start | bytes 786440 | tf_op jit(solution)/shard_map/ppermute | solution.py:222
  93.7 1.5 %shard_map.87 = (bf16[1,256,256]{2,1,0:T(8,128)(2,1)}, bf16[256,512]{1,0:T(8,128)(2,1)S(1)}) custom-call(bf16[512,256]{1,0:T(8,128)(2,1)S(1)} %shard_map.86.full_ref, s32[1,4]{1,0:T(1,128)S(1)} %copy-done.3), custom_call_target="tpu_custom_call" | custom-call | flops 67108864 | bytes 1048576 | tf_op jit(solution)/shard_map/pallas_call | solution.py:166
  95.2 6.4 %collective-permute-done.9.near_ref = bf16[512,256]{1,0:T(8,128)(2,1)S(1)} collective-permute-done((bf16[512,256]{1,0:T(8,128)(2,1)S(1)}, bf16[512,256]{1,0:T(8,128)(2,1)S(1)}, u32[]{:S(2)}, u32[]{:S(2)}) %collective-permute-start.9) | collective-permute-done | bytes 262176 | tf_op jit(solution)/shard_map/ppermute | solution.py:222
  101.5 0.9 shard_map.88
  (31 shorter events, 3.2 us)
Async XLA Ops:
  0.6 73.1 %copy-start = (bf16[1,4096,128]{2,1,0:T(8,128)(2,1)S(1)}, bf16[1,4096,128]{2,1,0:T(8,128)(2,1)}, u32[]{:S(2)}) copy-start(bf16[1,4096,128]{2,1,0:T(8,128)(2,1)} %param.8) | copy-start | bytes 3145732
  0.6 3.7 %copy-start.1 = (bf16[8,256,512]{2,1,0:T(8,128)(2,1)S(1)}, bf16[8,256,512]{2,1,0:T(8,128)(2,1)}, u32[]{:S(2)}) copy-start(bf16[8,256,512]{2,1,0:T(8,128)(2,1)} %param.6) | copy-start | bytes 6291460
  0.7 9.9 %copy-start.2 = (bf16[512,1024]{1,0:T(8,128)(2,1)S(1)}, bf16[512,1024]{1,0:T(8,128)(2,1)}, u32[]{:S(2)}) copy-start(bf16[512,1024]{1,0:T(8,128)(2,1)} %occ_hbm.1) | copy-start | bytes 3145732
  4.4 7.7 %collective-permute-start.4 = (bf16[2048,512]{1,0:T(8,128)(2,1)S(1)}, bf16[2048,512]{1,0:T(8,128)(2,1)S(1)}, u32[]{:S(2)}, u32[]{:S(2)}) collective-permute-start(bf16[2048,512]{1,0:T(8,128)(2,1)S(1)} %bitcast.10), channel_id=1, source_target_pairs={{0,8},{8,0},{16,24},{24,16},{32,40},{40,32},{48,56},{56,48},{64,72... | collective-permute-start | bytes 6291464 | tf_op jit(solution)/shard_map/ppermute | solution.py:31
  6.3 18.3 %collective-permute-start = (bf16[128,2048]{1,0:T(8,128)(2,1)}, bf16[128,2048]{1,0:T(8,128)(2,1)S(1)}, u32[]{:S(2)}, u32[]{:S(2)}) collective-permute-start(bf16[128,2048]{1,0:T(8,128)(2,1)} %shard_map.78), channel_id=1, source_target_pairs={{0,1},{1,2},{2,3},{3,4},{4,5},{5,6},{6,7},{7,0},{8,15},{9,8},{10,9... | collective-permute-start | bytes 1572872 | tf_op jit(solution)/shard_map/ppermute | solution.py:27
  12.9 17.3 %collective-permute-start.5 = (bf16[128,2048]{1,0:T(8,128)(2,1)S(1)}, bf16[128,2048]{1,0:T(8,128)(2,1)S(1)}, u32[]{:S(2)}, u32[]{:S(2)}) collective-permute-start(bf16[128,2048]{1,0:T(8,128)(2,1)S(1)} %shard_map.85), channel_id=1, source_target_pairs={{0,1},{1,2},{2,3},{3,4},{4,5},{5,6},{6,7},{7,0},{8,15},{9,8},{10,9... | collective-permute-start | bytes 1572872 | tf_op jit(solution)/shard_map/ppermute | solution.py:27
  24.7 12.3 %collective-permute-start.1 = (bf16[128,2048]{1,0:T(8,128)(2,1)S(1)}, bf16[128,2048]{1,0:T(8,128)(2,1)S(1)}, u32[]{:S(2)}, u32[]{:S(2)}) collective-permute-start(bf16[128,2048]{1,0:T(8,128)(2,1)S(1)} %add_convert_fusion.6), channel_id=1, source_target_pairs={{0,1},{1,2},{2,3},{3,4},{4,5},{5,6},{6,7},{7,0},{8,15},{9,8},{10,9... | collective-permute-start | bytes 1572872 | tf_op jit(solution)/shard_map/ppermute | solution.py:27
  30.4 12.3 %collective-permute-start.6 = (bf16[128,2048]{1,0:T(8,128)(2,1)S(1)}, bf16[128,2048]{1,0:T(8,128)(2,1)S(1)}, u32[]{:S(2)}, u32[]{:S(2)}) collective-permute-start(bf16[128,2048]{1,0:T(8,128)(2,1)S(1)} %add_convert_fusion.2), channel_id=1, source_target_pairs={{0,1},{1,2},{2,3},{3,4},{4,5},{5,6},{6,7},{7,0},{8,15},{9,8},{10,9... | collective-permute-start | bytes 1572872 | tf_op jit(solution)/shard_map/ppermute | solution.py:27
  37.1 12.3 %collective-permute-start.2 = (bf16[128,2048]{1,0:T(8,128)(2,1)S(1)}, bf16[128,2048]{1,0:T(8,128)(2,1)S(1)}, u32[]{:S(2)}, u32[]{:S(2)}) collective-permute-start(bf16[128,2048]{1,0:T(8,128)(2,1)S(1)} %add_convert_fusion.5), channel_id=1, source_target_pairs={{0,1},{1,2},{2,3},{3,4},{4,5},{5,6},{6,7},{7,0},{8,15},{9,8},{10,9... | collective-permute-start | bytes 1572872 | tf_op jit(solution)/shard_map/ppermute | solution.py:27
  42.8 12.3 %collective-permute-start.7 = (bf16[128,2048]{1,0:T(8,128)(2,1)S(1)}, bf16[128,2048]{1,0:T(8,128)(2,1)S(1)}, u32[]{:S(2)}, u32[]{:S(2)}) collective-permute-start(bf16[128,2048]{1,0:T(8,128)(2,1)S(1)} %add_convert_fusion.1), channel_id=1, source_target_pairs={{0,1},{1,2},{2,3},{3,4},{4,5},{5,6},{6,7},{7,0},{8,15},{9,8},{10,9... | collective-permute-start | bytes 1572872 | tf_op jit(solution)/shard_map/ppermute | solution.py:27
  49.6 12.3 %collective-permute-start.3 = (bf16[128,2048]{1,0:T(8,128)(2,1)S(1)}, bf16[128,2048]{1,0:T(8,128)(2,1)S(1)}, u32[]{:S(2)}, u32[]{:S(2)}) collective-permute-start(bf16[128,2048]{1,0:T(8,128)(2,1)S(1)} %add_convert_fusion.4), channel_id=1, source_target_pairs={{0,1},{1,2},{2,3},{3,4},{4,5},{5,6},{6,7},{7,0},{8,15},{9,8},{10,9... | collective-permute-start | bytes 1572872 | tf_op jit(solution)/shard_map/ppermute | solution.py:27
  55.1 6.8 %collective-permute-start.8 = (bf16[128,2048]{1,0:T(8,128)(2,1)S(1)}, bf16[128,2048]{1,0:T(8,128)(2,1)S(1)}, u32[]{:S(2)}, u32[]{:S(2)}) collective-permute-start(bf16[128,2048]{1,0:T(8,128)(2,1)S(1)} %collective-permute-done.7), channel_id=1, source_target_pairs={{0,8},{8,0},{16,24},{24,16},{32,40},{40,32},{48,56},{56,48},{64,72... | collective-permute-start | bytes 1572872 | tf_op jit(solution)/shard_map/ppermute | solution.py:31
  57.8 15.8 %copy-start.4 = (s32[4,16]{1,0:T(4,128)S(1)}, s32[4,16]{1,0:T(4,128)}, u32[]{:S(2)}) copy-start(s32[4,16]{1,0:T(4,128)} %param.11) | copy-start | bytes 772
  57.8 16.6 %copy-start.5 = (s32[1,256]{1,0:T(1,128)S(1)}, s32[1,256]{1,0:T(1,128)}, u32[]{:S(2)}) copy-start(s32[1,256]{1,0:T(1,128)} %param.9) | copy-start | bytes 3076
  63.0 30.7 %copy-start.3 = (s32[1,4]{1,0:T(1,128)S(1)}, s32[1,4]{1,0:T(1,128)}, u32[]{:S(2)}) copy-start(s32[1,4]{1,0:T(1,128)} %keep_ref.1) | copy-start | bytes 52
  63.0 28.4 %all-to-all-start = ((bf16[64,2,8,256]{3,2,1,0:T(8,128)(2,1)}), bf16[64,2,8,256]{3,2,1,0:T(8,128)(2,1)S(1)}, u32[]{:S(2)}, u32[]{:S(2)}) async-start(bf16[64,2,8,256]{3,2,1,0:T(8,128)(2,1)} %bitcast.5), calls=%async_computation | async-start | bytes 1048576 | tf_op jit(solution)/shard_map/all_to_all | solution.py:220
  91.7 9.8 %collective-permute-start.9 = (bf16[512,256]{1,0:T(8,128)(2,1)S(1)}, bf16[512,256]{1,0:T(8,128)(2,1)S(1)}, u32[]{:S(2)}, u32[]{:S(2)}) collective-permute-start(bf16[512,256]{1,0:T(8,128)(2,1)S(1)} %shard_map.86.full_ref), channel_id=1, source_target_pairs={{0,8},{8,16},{16,24},{24,32},{32,40},{40,48},{48,56},{56,64},{64,7... | collective-permute-start | bytes 786440 | tf_op jit(solution)/shard_map/ppermute | solution.py:222

commit v3 on v2

--- a/solution.py
+++ b/solution.py
@@ -14,16 +14,17 @@
 BF = jnp.bfloat16
 F32 = jnp.float32
 PARTS = 1
+HINT_B = 1000000
 FIRST_VMEM = 56 * 2**20
 VMEM_LIMIT = 16 * 2**20
 
 
-def hop(value, doms, ring):
+def hop(value, doms, ring, other=0):
     pairs = []
     for d in range(doms):
         step = 1 if d % 2 == 0 else -1
         for s in range(ring):
-            pairs.append((d * ring + s, d * ring + (s + step) % ring))
+            pairs.append((d * ring + s, (d ^ other) * ring + (s + step) % ring))
     return lax.ppermute(value, ("dom", "ao"), pairs)
 
 
@@ -189,6 +190,42 @@
     )(turned, near)
 
 
+def add_kernel(begin, x_ref, y_ref, out_ref):
+    width = y_ref.shape[1]
+    if begin > 0:
+        out_ref[:, :begin] = x_ref[:, :begin]
+    if begin + width < x_ref.shape[1]:
+        out_ref[:, begin + width :] = x_ref[:, begin + width :]
+    part = slice(begin, begin + width)
+    out_ref[:, part] = (x_ref[:, part].astype(F32) + y_ref[...].astype(F32)).astype(BF)
+
+
+def steer_add(x, y, flops, begin=0):
+    return pl.pallas_call(
+        functools.partial(add_kernel, begin),
+        out_shape=jax.ShapeDtypeStruct(x.shape, BF),
+        in_specs=[vm, vm],
+        out_specs=vm,
+        compiler_params=pltpu.CompilerParams(vmem_limit_bytes=VMEM_LIMIT),
+        cost_estimate=cost(flops, 6 * x.size),
+    )(x, y)
+
+
+def after_kernel(x_ref, y_ref, after_ref, out_ref):
+    out_ref[...] = (x_ref[...].astype(F32) + y_ref[...].astype(F32)).astype(BF)
+
+
+def after_add(x, y, after):
+    return pl.pallas_call(
+        after_kernel,
+        out_shape=jax.ShapeDtypeStruct(x.shape, BF),
+        in_specs=[vm, vm, pl.BlockSpec(memory_space=pl.ANY)],
+        out_specs=vm,
+        compiler_params=pltpu.CompilerParams(vmem_limit_bytes=VMEM_LIMIT),
+        cost_estimate=cost(x.size, 6 * x.size),
+    )(x, y, after)
+
+
 def body(three_index, occ_coef, pao_coef, ao_map, aux_map, ao_list):
     doms, ring = lax.axis_size("dom"), lax.axis_size("ao")
     aux_rows, mu_rows, nu_local = three_index.shape
@@ -203,14 +240,18 @@
     other = None
     half_ring = ring // 2
     for i in range(half_ring):
-        own = [add(t, hop(v, doms, ring)) for t, v in zip(term(w, i, slab), own)]
+        if i == 0:
+            other = term(w, i, other_slab)
+        own = [hop(v, doms, ring) for v in own]
+        if i == 0:
+            own = [after_add(t, v, o) for t, v, o in zip(term(w, i, slab), own, other)]
+        else:
+            own = [add(t, v) for t, v in zip(term(w, i, slab), own)]
         if i < half_ring - 1:
-            if i == 0:
-                other = term(w, i, other_slab)
-            else:
-                other = [add(t, v) for t, v in zip(term(w, i, other_slab), other)]
-            other = [hop(v, doms, ring) for v in other]
-    halves = [add(v, swap(o, doms)) for v, o in zip(own, other)]
+            if i > 0:
+                other = [steer_add(t, v, HINT_B) for t, v in zip(term(w, i, other_slab), other)]
+            other = [hop(v, doms, ring, 1 if i == half_ring - 2 else 0) for v in other]
+    halves = [add(v, o) for v, o in zip(own, other)]
 
     shells = pao_coef[0].reshape(-1, AOB, pao_d)
     keep = ao_map[0].astype(BF)[ao_list]

time: 103 us -> 103 us (level)
  starting transfers between devices: 34.5 us -> 32.6 us
  waiting for transfers between devices: 49.7 us -> 51.6 us
    ppermute x7, waiting for transfers between devices: 27.5 us -> 29.4 us  [hop(): return lax.ppermute(value, ('dom', 'ao'), pairs)]
    ppermute x2 -> x1, starting transfers between devices: 3.83 us -> 1.92 us  [swap(): return lax.ppermute(value, 'dom', [(d, d ^ 1) for d in range(doms)])]
  transfers between devices with their start and end apart: 11 -> 10, of which waited for: 9 -> 9; matrix products, arithmetic and copies ran while one was open for 3% -> 2% of each run, Pallas kernels for 8% -> 9%
where the time goes in v3:
time: 103 us; the launch traced here: 102 us
  waiting for transfers between devices  51.6 us (50%)
  starting transfers between devices  32.6 us (32%)
  Pallas kernels  13.9 us (13%)
  local copies, waits for them, and re-layouts  2.69 us (3%)
    ppermute x7, waiting for transfers between devices, hop(): return lax.ppermute(value, ('dom', 'ao'), pairs)  29.4 us
    ppermute x7, starting transfers between devices, hop(): return lax.ppermute(value, ('dom', 'ao'), pairs)  18.2 us
    all_to_all x1, waiting for transfers between devices, body(): got = lax.all_to_all(half, 'dom', split_axis=0, concat_axis=0, tiled=True)  15.8 us
    all_to_all x1, starting transfers between devices, body(): got = lax.all_to_all(half, 'dom', split_axis=0, concat_axis=0, tiled=True)  10.6 us
    ppermute x1, waiting for transfers between devices, body(): near = lax.ppermute(full, 'dom', [(d, (d + 1) % doms) for d in range(doms)])  6.36 us
    pallas_call x7, Pallas kernels, term(): pl.pallas_call(term_kernel, grid=(1,), out_shape=[jax.ShapeDtypeStruct((r...  5.67 us
    pallas_call x1, Pallas kernels, first_term(): pl.pallas_call(functools.partial(first_kernel, ring), out_shape=[jax.Shap...  3.67 us
  transfers between devices with their start and end apart: 10, of which 9 were waited for; matrix products, arithmetic and copies ran while one was open for 2% of the time, Pallas kernels for 9%

profile of v3, /device:TPU:16, one launch (start us, length us, event | category | flops | bytes accessed | tf_op | source)
XLA Modules:
  0.0 102.4 jit_solution(10180861924428189611)
XLA Ops:
  0.7 3.7 %shard_map.78 = bf16[128,2048]{1,0:T(8,128)(2,1)} custom-call(bf16[512,1024]{1,0:T(8,128)(2,1)} %occ_hbm.1, bf16[2048,512]{1,0:T(8,128)(2,1)} %bitcast.9), custom_call_target="tpu_custom_call" | custom-call | flops 268435456 | bytes 3145728 | tf_op jit(solution)/shard_map/pallas_call | solution.py:70
  4.4 1.9 %collective-permute-start.1 = (bf16[2048,512]{1,0:T(8,128)(2,1)S(1)}, bf16[2048,512]{1,0:T(8,128)(2,1)S(1)}, u32[]{:S(2)}, u32[]{:S(2)}) collective-permute-start(bf16[2048,512]{1,0:T(8,128)(2,1)S(1)} %bitcast.10), channel_id=1, source_target_pairs={{0,8},{8,0},{16,24},{24,16},{32,40},{40,32},{48,56},{56,48},{64,72... | collective-permute-start | bytes 6291464 | tf_op jit(solution)/shard_map/ppermute | solution.py:32
  6.3 4.3 %collective-permute-start = (bf16[128,2048]{1,0:T(8,128)(2,1)}, bf16[128,2048]{1,0:T(8,128)(2,1)S(1)}, u32[]{:S(2)}, u32[]{:S(2)}) collective-permute-start(bf16[128,2048]{1,0:T(8,128)(2,1)} %shard_map.78), channel_id=1, source_target_pairs={{0,1},{1,2},{2,3},{3,4},{4,5},{5,6},{6,7},{7,0},{8,15},{9,8},{10,9... | collective-permute-start | bytes 1572872 | tf_op jit(solution)/shard_map/ppermute | solution.py:28
  10.6 1.5 %shard_map.77.w_ref = bf16[4,128,512]{2,1,0:T(8,128)(2,1)S(1)} custom-call(bf16[512,1024]{1,0:T(8,128)(2,1)S(1)} %copy-done.2), custom_call_target="tpu_custom_call" | custom-call | flops 536870912 | bytes 2097152 | tf_op jit(solution)/shard_map/pallas_call | solution.py:94
  12.1 0.8 shard_map.83.after_ref
  12.9 4.3 %collective-permute-start.5 = (bf16[128,2048]{1,0:T(8,128)(2,1)S(1)}, bf16[128,2048]{1,0:T(8,128)(2,1)S(1)}, u32[]{:S(2)}, u32[]{:S(2)}) collective-permute-start(bf16[128,2048]{1,0:T(8,128)(2,1)S(1)} %shard_map.83.after_ref), channel_id=1, source_target_pairs={{0,1},{1,2},{2,3},{3,4},{4,5},{5,6},{6,7},{7,0},{8,15},{9,8},{10,9... | collective-permute-start | bytes 1572872 | tf_op jit(solution)/shard_map/ppermute | solution.py:28
  17.2 0.8 shard_map.82.x_ref
  18.0 6.6 %collective-permute-done.y_ref = bf16[128,2048]{1,0:T(8,128)(2,1)S(1)} collective-permute-done((bf16[128,2048]{1,0:T(8,128)(2,1)}, bf16[128,2048]{1,0:T(8,128)(2,1)S(1)}, u32[]{:S(2)}, u32[]{:S(2)}) %collective-permute-start) | collective-permute-done | bytes 524320 | tf_op jit(solution)/shard_map/ppermute | solution.py:28
  24.7 1.9 %collective-permute-start.2 = (bf16[128,2048]{1,0:T(8,128)(2,1)S(1)}, bf16[128,2048]{1,0:T(8,128)(2,1)S(1)}, u32[]{:S(2)}, u32[]{:S(2)}) collective-permute-start(bf16[128,2048]{1,0:T(8,128)(2,1)S(1)} %shard_map.84), channel_id=1, source_target_pairs={{0,1},{1,2},{2,3},{3,4},{4,5},{5,6},{6,7},{7,0},{8,15},{9,8},{10,9... | collective-permute-start | bytes 1572872 | tf_op jit(solution)/shard_map/ppermute | solution.py:28
  26.7 0.8 shard_map.81
  27.5 0.8 shard_map.86.x_ref
  28.3 1.9 %collective-permute-done.5.y_ref = bf16[128,2048]{1,0:T(8,128)(2,1)S(1)} collective-permute-done((bf16[128,2048]{1,0:T(8,128)(2,1)S(1)}, bf16[128,2048]{1,0:T(8,128)(2,1)S(1)}, u32[]{:S(2)}, u32[]{:S(2)}) %collective-permute-start.5) | collective-permute-done | bytes 524320 | tf_op jit(solution)/shard_map/ppermute | solution.py:28
  30.3 1.9 %collective-permute-start.6 = (bf16[128,2048]{1,0:T(8,128)(2,1)S(1)}, bf16[128,2048]{1,0:T(8,128)(2,1)S(1)}, u32[]{:S(2)}, u32[]{:S(2)}) collective-permute-start(bf16[128,2048]{1,0:T(8,128)(2,1)S(1)} %shard_map.87), channel_id=1, source_target_pairs={{0,1},{1,2},{2,3},{3,4},{4,5},{5,6},{6,7},{7,0},{8,15},{9,8},{10,9... | collective-permute-start | bytes 1572872 | tf_op jit(solution)/shard_map/ppermute | solution.py:28
  32.3 4.7 %collective-permute-done.2 = bf16[128,2048]{1,0:T(8,128)(2,1)S(1)} collective-permute-done((bf16[128,2048]{1,0:T(8,128)(2,1)S(1)}, bf16[128,2048]{1,0:T(8,128)(2,1)S(1)}, u32[]{:S(2)}, u32[]{:S(2)}) %collective-permute-start.2) | collective-permute-done | bytes 524320 | tf_op jit(solution)/shard_map/ppermute | solution.py:28
  37.1 1.9 %collective-permute-start.3 = (bf16[128,2048]{1,0:T(8,128)(2,1)S(1)}, bf16[128,2048]{1,0:T(8,128)(2,1)S(1)}, u32[]{:S(2)}, u32[]{:S(2)}) collective-permute-start(bf16[128,2048]{1,0:T(8,128)(2,1)S(1)} %add_convert_fusion.3), channel_id=1, source_target_pairs={{0,1},{1,2},{2,3},{3,4},{4,5},{5,6},{6,7},{7,0},{8,15},{9,8},{10,9... | collective-permute-start | bytes 1572872 | tf_op jit(solution)/shard_map/ppermute | solution.py:28
  39.1 0.8 shard_map.80
  39.9 0.8 shard_map.85.x_ref
  40.7 1.9 %collective-permute-done.6.y_ref = bf16[128,2048]{1,0:T(8,128)(2,1)S(1)} collective-permute-done((bf16[128,2048]{1,0:T(8,128)(2,1)S(1)}, bf16[128,2048]{1,0:T(8,128)(2,1)S(1)}, u32[]{:S(2)}, u32[]{:S(2)}) %collective-permute-start.6) | collective-permute-done | bytes 524320 | tf_op jit(solution)/shard_map/ppermute | solution.py:28
  42.8 1.9 %collective-permute-start.7 = (bf16[128,2048]{1,0:T(8,128)(2,1)S(1)}, bf16[128,2048]{1,0:T(8,128)(2,1)S(1)}, u32[]{:S(2)}, u32[]{:S(2)}) collective-permute-start(bf16[128,2048]{1,0:T(8,128)(2,1)S(1)} %shard_map.88), channel_id=1, source_target_pairs={{0,9},{1,10},{2,11},{3,12},{4,13},{5,14},{6,15},{7,8},{8,7},{9,0},... | collective-permute-start | bytes 1572872 | tf_op jit(solution)/shard_map/ppermute | solution.py:28
  44.7 4.7 %collective-permute-done.3 = bf16[128,2048]{1,0:T(8,128)(2,1)S(1)} collective-permute-done((bf16[128,2048]{1,0:T(8,128)(2,1)S(1)}, bf16[128,2048]{1,0:T(8,128)(2,1)S(1)}, u32[]{:S(2)}, u32[]{:S(2)}) %collective-permute-start.3) | collective-permute-done | bytes 524320 | tf_op jit(solution)/shard_map/ppermute | solution.py:28
  49.6 1.9 %collective-permute-start.4 = (bf16[128,2048]{1,0:T(8,128)(2,1)S(1)}, bf16[128,2048]{1,0:T(8,128)(2,1)S(1)}, u32[]{:S(2)}, u32[]{:S(2)}) collective-permute-start(bf16[128,2048]{1,0:T(8,128)(2,1)S(1)} %add_convert_fusion.2), channel_id=1, source_target_pairs={{0,1},{1,2},{2,3},{3,4},{4,5},{5,6},{6,7},{7,0},{8,15},{9,8},{10,9... | collective-permute-start | bytes 1572872 | tf_op jit(solution)/shard_map/ppermute | solution.py:28
  51.5 0.8 shard_map.79
  52.3 0.9 collective-permute-done.7
  53.3 8.6 %collective-permute-done.4 = bf16[128,2048]{1,0:T(8,128)(2,1)S(1)} collective-permute-done((bf16[128,2048]{1,0:T(8,128)(2,1)S(1)}, bf16[128,2048]{1,0:T(8,128)(2,1)S(1)}, u32[]{:S(2)}, u32[]{:S(2)}) %collective-permute-start.4) | collective-permute-done | bytes 524320 | tf_op jit(solution)/shard_map/ppermute | solution.py:28
  62.1 0.9 copy.8
  63.0 10.6 %all-to-all-start = ((bf16[64,2,8,256]{3,2,1,0:T(8,128)(2,1)}), bf16[64,2,8,256]{3,2,1,0:T(8,128)(2,1)S(1)}, u32[]{:S(2)}, u32[]{:S(2)}) async-start(bf16[64,2,8,256]{3,2,1,0:T(8,128)(2,1)} %bitcast.5), calls=%async_computation | async-start | bytes 1048576 | tf_op jit(solution)/shard_map/all_to_all | solution.py:261
  73.7 0.8 gather_fusion.1
  75.6 15.8 %all-to-all-done.got_ref = bf16[64,2,8,256]{3,2,1,0:T(8,128)(2,1)S(1)} async-done(((bf16[64,2,8,256]{3,2,1,0:T(8,128)(2,1)}), bf16[64,2,8,256]{3,2,1,0:T(8,128)(2,1)S(1)}, u32[]{:S(2)}, u32[]{:S(2)}) %all-to-all-start) | async-done | bytes 524320 | tf_op jit(solution)/shard_map/all_to_all | solution.py:261
  91.7 1.9 %collective-permute-start.8 = (bf16[512,256]{1,0:T(8,128)(2,1)S(1)}, bf16[512,256]{1,0:T(8,128)(2,1)S(1)}, u32[]{:S(2)}, u32[]{:S(2)}) collective-permute-start(bf16[512,256]{1,0:T(8,128)(2,1)S(1)} %shard_map.89.full_ref), channel_id=1, source_target_pairs={{0,8},{8,16},{16,24},{24,32},{32,40},{40,48},{48,56},{56,64},{64,7... | collective-permute-start | bytes 786440 | tf_op jit(solution)/shard_map/ppermute | solution.py:263
  93.7 1.5 %shard_map.90 = (bf16[1,256,256]{2,1,0:T(8,128)(2,1)}, bf16[256,512]{1,0:T(8,128)(2,1)S(1)}) custom-call(bf16[512,256]{1,0:T(8,128)(2,1)S(1)} %shard_map.89.full_ref, s32[1,4]{1,0:T(1,128)S(1)} %copy-done.3), custom_call_target="tpu_custom_call" | custom-call | flops 67108864 | bytes 1048576 | tf_op jit(solution)/shard_map/pallas_call | solution.py:167
  95.2 6.4 %collective-permute-done.8.near_ref = bf16[512,256]{1,0:T(8,128)(2,1)S(1)} collective-permute-done((bf16[512,256]{1,0:T(8,128)(2,1)S(1)}, bf16[512,256]{1,0:T(8,128)(2,1)S(1)}, u32[]{:S(2)}, u32[]{:S(2)}) %collective-permute-start.8) | collective-permute-done | bytes 262176 | tf_op jit(solution)/shard_map/ppermute | solution.py:263
  101.5 0.9 shard_map.91
  (29 shorter events, 2.4 us)
Async XLA Ops:
  0.6 74.1 %copy-start = (bf16[1,4096,128]{2,1,0:T(8,128)(2,1)S(1)}, bf16[1,4096,128]{2,1,0:T(8,128)(2,1)}, u32[]{:S(2)}) copy-start(bf16[1,4096,128]{2,1,0:T(8,128)(2,1)} %param.8) | copy-start | bytes 3145732
  0.6 9.9 %copy-start.2 = (bf16[512,1024]{1,0:T(8,128)(2,1)S(1)}, bf16[512,1024]{1,0:T(8,128)(2,1)}, u32[]{:S(2)}) copy-start(bf16[512,1024]{1,0:T(8,128)(2,1)} %occ_hbm.1) | copy-start | bytes 3145732
  0.7 3.7 %copy-start.1 = (bf16[8,256,512]{2,1,0:T(8,128)(2,1)S(1)}, bf16[8,256,512]{2,1,0:T(8,128)(2,1)}, u32[]{:S(2)}) copy-start(bf16[8,256,512]{2,1,0:T(8,128)(2,1)} %param.6) | copy-start | bytes 6291460
  4.4 7.7 %collective-permute-start.1 = (bf16[2048,512]{1,0:T(8,128)(2,1)S(1)}, bf16[2048,512]{1,0:T(8,128)(2,1)S(1)}, u32[]{:S(2)}, u32[]{:S(2)}) collective-permute-start(bf16[2048,512]{1,0:T(8,128)(2,1)S(1)} %bitcast.10), channel_id=1, source_target_pairs={{0,8},{8,0},{16,24},{24,16},{32,40},{40,32},{48,56},{56,48},{64,72... | collective-permute-start | bytes 6291464 | tf_op jit(solution)/shard_map/ppermute | solution.py:32
  6.3 18.3 %collective-permute-start = (bf16[128,2048]{1,0:T(8,128)(2,1)}, bf16[128,2048]{1,0:T(8,128)(2,1)S(1)}, u32[]{:S(2)}, u32[]{:S(2)}) collective-permute-start(bf16[128,2048]{1,0:T(8,128)(2,1)} %shard_map.78), channel_id=1, source_target_pairs={{0,1},{1,2},{2,3},{3,4},{4,5},{5,6},{6,7},{7,0},{8,15},{9,8},{10,9... | collective-permute-start | bytes 1572872 | tf_op jit(solution)/shard_map/ppermute | solution.py:28
  12.9 17.3 %collective-permute-start.5 = (bf16[128,2048]{1,0:T(8,128)(2,1)S(1)}, bf16[128,2048]{1,0:T(8,128)(2,1)S(1)}, u32[]{:S(2)}, u32[]{:S(2)}) collective-permute-start(bf16[128,2048]{1,0:T(8,128)(2,1)S(1)} %shard_map.83.after_ref), channel_id=1, source_target_pairs={{0,1},{1,2},{2,3},{3,4},{4,5},{5,6},{6,7},{7,0},{8,15},{9,8},{10,9... | collective-permute-start | bytes 1572872 | tf_op jit(solution)/shard_map/ppermute | solution.py:28
  24.7 12.3 %collective-permute-start.2 = (bf16[128,2048]{1,0:T(8,128)(2,1)S(1)}, bf16[128,2048]{1,0:T(8,128)(2,1)S(1)}, u32[]{:S(2)}, u32[]{:S(2)}) collective-permute-start(bf16[128,2048]{1,0:T(8,128)(2,1)S(1)} %shard_map.84), channel_id=1, source_target_pairs={{0,1},{1,2},{2,3},{3,4},{4,5},{5,6},{6,7},{7,0},{8,15},{9,8},{10,9... | collective-permute-start | bytes 1572872 | tf_op jit(solution)/shard_map/ppermute | solution.py:28
  30.3 12.3 %collective-permute-start.6 = (bf16[128,2048]{1,0:T(8,128)(2,1)S(1)}, bf16[128,2048]{1,0:T(8,128)(2,1)S(1)}, u32[]{:S(2)}, u32[]{:S(2)}) collective-permute-start(bf16[128,2048]{1,0:T(8,128)(2,1)S(1)} %shard_map.87), channel_id=1, source_target_pairs={{0,1},{1,2},{2,3},{3,4},{4,5},{5,6},{6,7},{7,0},{8,15},{9,8},{10,9... | collective-permute-start | bytes 1572872 | tf_op jit(solution)/shard_map/ppermute | solution.py:28
  37.1 12.3 %collective-permute-start.3 = (bf16[128,2048]{1,0:T(8,128)(2,1)S(1)}, bf16[128,2048]{1,0:T(8,128)(2,1)S(1)}, u32[]{:S(2)}, u32[]{:S(2)}) collective-permute-start(bf16[128,2048]{1,0:T(8,128)(2,1)S(1)} %add_convert_fusion.3), channel_id=1, source_target_pairs={{0,1},{1,2},{2,3},{3,4},{4,5},{5,6},{6,7},{7,0},{8,15},{9,8},{10,9... | collective-permute-start | bytes 1572872 | tf_op jit(solution)/shard_map/ppermute | solution.py:28
  42.8 10.5 %collective-permute-start.7 = (bf16[128,2048]{1,0:T(8,128)(2,1)S(1)}, bf16[128,2048]{1,0:T(8,128)(2,1)S(1)}, u32[]{:S(2)}, u32[]{:S(2)}) collective-permute-start(bf16[128,2048]{1,0:T(8,128)(2,1)S(1)} %shard_map.88), channel_id=1, source_target_pairs={{0,9},{1,10},{2,11},{3,12},{4,13},{5,14},{6,15},{7,8},{8,7},{9,0},... | collective-permute-start | bytes 1572872 | tf_op jit(solution)/shard_map/ppermute | solution.py:28
  49.6 12.3 %collective-permute-start.4 = (bf16[128,2048]{1,0:T(8,128)(2,1)S(1)}, bf16[128,2048]{1,0:T(8,128)(2,1)S(1)}, u32[]{:S(2)}, u32[]{:S(2)}) collective-permute-start(bf16[128,2048]{1,0:T(8,128)(2,1)S(1)} %add_convert_fusion.2), channel_id=1, source_target_pairs={{0,1},{1,2},{2,3},{3,4},{4,5},{5,6},{6,7},{7,0},{8,15},{9,8},{10,9... | collective-permute-start | bytes 1572872 | tf_op jit(solution)/shard_map/ppermute | solution.py:28
  52.3 21.3 %copy-start.4 = (s32[4,16]{1,0:T(4,128)S(1)}, s32[4,16]{1,0:T(4,128)}, u32[]{:S(2)}) copy-start(s32[4,16]{1,0:T(4,128)} %param.11) | copy-start | bytes 772
  52.3 21.4 %copy-start.5 = (s32[1,256]{1,0:T(1,128)S(1)}, s32[1,256]{1,0:T(1,128)}, u32[]{:S(2)}) copy-start(s32[1,256]{1,0:T(1,128)} %param.9) | copy-start | bytes 3076
  63.0 30.6 %copy-start.3 = (s32[1,4]{1,0:T(1,128)S(1)}, s32[1,4]{1,0:T(1,128)}, u32[]{:S(2)}) copy-start(s32[1,4]{1,0:T(1,128)} %keep_ref.1) | copy-start | bytes 52
  63.0 28.4 %all-to-all-start = ((bf16[64,2,8,256]{3,2,1,0:T(8,128)(2,1)}), bf16[64,2,8,256]{3,2,1,0:T(8,128)(2,1)S(1)}, u32[]{:S(2)}, u32[]{:S(2)}) async-start(bf16[64,2,8,256]{3,2,1,0:T(8,128)(2,1)} %bitcast.5), calls=%async_computation | async-start | bytes 1048576 | tf_op jit(solution)/shard_map/all_to_all | solution.py:261
  91.7 9.8 %collective-permute-start.8 = (bf16[512,256]{1,0:T(8,128)(2,1)S(1)}, bf16[512,256]{1,0:T(8,128)(2,1)S(1)}, u32[]{:S(2)}, u32[]{:S(2)}) collective-permute-start(bf16[512,256]{1,0:T(8,128)(2,1)S(1)} %shard_map.89.full_ref), channel_id=1, source_target_pairs={{0,8},{8,16},{16,24},{24,32},{32,40},{40,48},{48,56},{56,64},{64,7... | collective-permute-start | bytes 786440 | tf_op jit(solution)/shard_map/ppermute | solution.py:263

commit v4 on v3

--- a/solution.py
+++ b/solution.py
@@ -61,15 +61,15 @@
     w = pick_rows(occ_ref[...], out_refs[0].shape[0], ring, ring // 2)
     for c in range(PARTS):
         slab_copies[c].wait()
-        out_refs[c][...] = nt(w, slab_ref[c * cut : (c + 1) * cut]).astype(BF)
-
-
-def first_term(occ, slab, ring):
+        out_refs[c][...] = nt(w, slab_ref[c * cut : (c + 1) * cut]).reshape(out_refs[c].shape).astype(BF)
+
+
+def first_term(occ, slab, ring, aux_rows):
     rows, width = occ.shape[1] // ring, slab.shape[0] // PARTS
     vm, hbm = pl.BlockSpec(memory_space=pltpu.VMEM), pl.BlockSpec(memory_space=pl.ANY)
     return pl.pallas_call(
         functools.partial(first_kernel, ring),
-        out_shape=[jax.ShapeDtypeStruct((rows, width), BF)] * PARTS,
+        out_shape=[jax.ShapeDtypeStruct((rows, aux_rows // PARTS, width * PARTS // aux_rows), BF)] * PARTS,
         in_specs=[hbm, hbm],
         out_specs=[vm] * PARTS,
         scratch_shapes=[
@@ -104,16 +104,16 @@
 def term_kernel(w_ref, slab_ref, *out_refs):
     cut = slab_ref.shape[0] // PARTS
     for c in range(PARTS):
-        out_refs[c][...] = nt(w_ref[0], slab_ref[c * cut : (c + 1) * cut]).astype(BF)
-
-
-def term(w, i, slab):
+        out_refs[c][...] = nt(w_ref[0], slab_ref[c * cut : (c + 1) * cut]).reshape(out_refs[c].shape).astype(BF)
+
+
+def term(w, i, slab, aux_rows):
     rows, width = w.shape[1], slab.shape[0] // PARTS
     vm = pl.BlockSpec(memory_space=pltpu.VMEM)
     return pl.pallas_call(
         term_kernel,
         grid=(1,),
-        out_shape=[jax.ShapeDtypeStruct((rows, width), BF)] * PARTS,
+        out_shape=[jax.ShapeDtypeStruct((rows, aux_rows // PARTS, width * PARTS // aux_rows), BF)] * PARTS,
         in_specs=[pl.BlockSpec((1,) + w.shape[1:], lambda g: (i, 0, 0)), vm],
         out_specs=[vm] * PARTS,
         compiler_params=pltpu.CompilerParams(vmem_limit_bytes=VMEM_LIMIT),
@@ -190,19 +190,13 @@
     )(turned, near)
 
 
-def add_kernel(begin, x_ref, y_ref, out_ref):
-    width = y_ref.shape[1]
-    if begin > 0:
-        out_ref[:, :begin] = x_ref[:, :begin]
-    if begin + width < x_ref.shape[1]:
-        out_ref[:, begin + width :] = x_ref[:, begin + width :]
-    part = slice(begin, begin + width)
-    out_ref[:, part] = (x_ref[:, part].astype(F32) + y_ref[...].astype(F32)).astype(BF)
-
-
-def steer_add(x, y, flops, begin=0):
-    return pl.pallas_call(
-        functools.partial(add_kernel, begin),
+def add_kernel(x_ref, y_ref, out_ref):
+    out_ref[...] = (x_ref[...].astype(F32) + y_ref[...].astype(F32)).astype(BF)
+
+
+def steer_add(x, y, flops):
+    return pl.pallas_call(
+        add_kernel,
         out_shape=jax.ShapeDtypeStruct(x.shape, BF),
         in_specs=[vm, vm],
         out_specs=vm,
@@ -233,7 +227,7 @@
     pao_d = pao_coef.shape[2]
     slab = three_index.reshape(aux_rows * mu_rows, nu_local)
 
-    own = first_term(occ_coef, slab, ring)
+    own = first_term(occ_coef, slab, ring, aux_rows)
     w = pick_rest(occ_coef, ring)
     slab, own = lax.optimization_barrier((slab, own))
     other_slab = swap(slab, doms)
@@ -241,15 +235,15 @@
     half_ring = ring // 2
     for i in range(half_ring):
         if i == 0:
-            other = term(w, i, other_slab)
+            other = term(w, i, other_slab, aux_rows)
         own = [hop(v, doms, ring) for v in own]
         if i == 0:
-            own = [after_add(t, v, o) for t, v, o in zip(term(w, i, slab), own, other)]
+            own = [after_add(t, v, o) for t, v, o in zip(term(w, i, slab, aux_rows), own, other)]
         else:
-            own = [add(t, v) for t, v in zip(term(w, i, slab), own)]
+            own = [add(t, v) for t, v in zip(term(w, i, slab, aux_rows), own)]
         if i < half_ring - 1:
             if i > 0:
-                other = [steer_add(t, v, HINT_B) for t, v in zip(term(w, i, other_slab), other)]
+                other = [steer_add(t, v, HINT_B) for t, v in zip(term(w, i, other_slab, aux_rows), other)]
             other = [hop(v, doms, ring, 1 if i == half_ring - 2 else 0) for v in other]
     halves = [add(v, o) for v, o in zip(own, other)]
 

time: 103 us -> 103 us (level)
  no operation moved by 1% of the time
where the time goes in v4:
time: 103 us; the launch traced here: 102 us
  waiting for transfers between devices  50.9 us (49%)
  starting transfers between devices  32.6 us (32%)
  Pallas kernels  14.6 us (14%)
  local copies, waits for them, and re-layouts  1.79 us (2%)
  other arithmetic  1.47 us (1%)
    ppermute x7, waiting for transfers between devices, hop(): return lax.ppermute(value, ('dom', 'ao'), pairs)  28.7 us
    ppermute x7, starting transfers between devices, hop(): return lax.ppermute(value, ('dom', 'ao'), pairs)  18.2 us
    all_to_all x1, waiting for transfers between devices, body(): got = lax.all_to_all(half, 'dom', split_axis=0, concat_axis=0, tiled=True)  15.8 us
    all_to_all x1, starting transfers between devices, body(): got = lax.all_to_all(half, 'dom', split_axis=0, concat_axis=0, tiled=True)  10.6 us
    ppermute x1, waiting for transfers between devices, body(): near = lax.ppermute(full, 'dom', [(d, (d + 1) % doms) for d in range(doms)])  6.36 us
    pallas_call x7, Pallas kernels, term(): pl.pallas_call(term_kernel, grid=(1,), out_shape=[jax.ShapeDtypeStruct((r...  6.35 us
    pallas_call x1, Pallas kernels, first_term(): pl.pallas_call(functools.partial(first_kernel, ring), out_shape=[jax.Shap...  3.77 us
  transfers between devices with their start and end apart: 10, of which 9 were waited for; matrix products, arithmetic and copies ran while one was open for 2% of the time, Pallas kernels for 9%

profile of v4, /device:TPU:16, one launch (start us, length us, event | category | flops | bytes accessed | tf_op | source)
XLA Modules:
  0.0 102.3 jit_solution(16452670770874626732)
XLA Ops:
  0.7 3.8 %shard_map.78 = bf16[128,8,256]{2,1,0:T(8,128)(2,1)} custom-call(bf16[512,1024]{1,0:T(8,128)(2,1)} %occ_hbm.1, bf16[2048,512]{1,0:T(8,128)(2,1)} %bitcast.7), custom_call_target="tpu_custom_call" | custom-call | flops 268435456 | bytes 3145728 | tf_op jit(solution)/shard_map/pallas_call | solution.py:70
  4.5 1.9 %collective-permute-start.1 = (bf16[2048,512]{1,0:T(8,128)(2,1)S(1)}, bf16[2048,512]{1,0:T(8,128)(2,1)S(1)}, u32[]{:S(2)}, u32[]{:S(2)}) collective-permute-start(bf16[2048,512]{1,0:T(8,128)(2,1)S(1)} %bitcast.8), channel_id=1, source_target_pairs={{0,8},{8,0},{16,24},{24,16},{32,40},{40,32},{48,56},{56,48},{64,72... | collective-permute-start | bytes 6291464 | tf_op jit(solution)/shard_map/ppermute | solution.py:32
  6.4 4.3 %collective-permute-start = (bf16[128,8,256]{2,1,0:T(8,128)(2,1)}, bf16[128,8,256]{2,1,0:T(8,128)(2,1)S(1)}, u32[]{:S(2)}, u32[]{:S(2)}) collective-permute-start(bf16[128,8,256]{2,1,0:T(8,128)(2,1)} %shard_map.78), channel_id=1, source_target_pairs={{0,1},{1,2},{2,3},{3,4},{4,5},{5,6},{6,7},{7,0},{8,15},{9,8},{10,9... | collective-permute-start | bytes 1572872 | tf_op jit(solution)/shard_map/ppermute | solution.py:28
  10.7 1.5 %shard_map.77.w_ref = bf16[4,128,512]{2,1,0:T(8,128)(2,1)S(1)} custom-call(bf16[512,1024]{1,0:T(8,128)(2,1)S(1)} %copy-done.2), custom_call_target="tpu_custom_call" | custom-call | flops 536870912 | bytes 2097152 | tf_op jit(solution)/shard_map/pallas_call | solution.py:94
  12.2 0.9 shard_map.83.after_ref
  13.1 4.3 %collective-permute-start.5 = (bf16[128,8,256]{2,1,0:T(8,128)(2,1)S(1)}, bf16[128,8,256]{2,1,0:T(8,128)(2,1)S(1)}, u32[]{:S(2)}, u32[]{:S(2)}) collective-permute-start(bf16[128,8,256]{2,1,0:T(8,128)(2,1)S(1)} %shard_map.83.after_ref), channel_id=1, source_target_pairs={{0,1},{1,2},{2,3},{3,4},{4,5},{5,6},{6,7},{7,0},{8,15},{9,8},{10,9... | collective-permute-start | bytes 1572872 | tf_op jit(solution)/shard_map/ppermute | solution.py:28
  17.4 0.9 shard_map.82.x_ref
  18.3 6.4 %collective-permute-done.y_ref = bf16[128,8,256]{2,1,0:T(8,128)(2,1)S(1)} collective-permute-done((bf16[128,8,256]{2,1,0:T(8,128)(2,1)}, bf16[128,8,256]{2,1,0:T(8,128)(2,1)S(1)}, u32[]{:S(2)}, u32[]{:S(2)}) %collective-permute-start) | collective-permute-done | bytes 524320 | tf_op jit(solution)/shard_map/ppermute | solution.py:28
  24.8 1.9 %collective-permute-start.2 = (bf16[128,8,256]{2,1,0:T(8,128)(2,1)S(1)}, bf16[128,8,256]{2,1,0:T(8,128)(2,1)S(1)}, u32[]{:S(2)}, u32[]{:S(2)}) collective-permute-start(bf16[128,8,256]{2,1,0:T(8,128)(2,1)S(1)} %shard_map.84), channel_id=1, source_target_pairs={{0,1},{1,2},{2,3},{3,4},{4,5},{5,6},{6,7},{7,0},{8,15},{9,8},{10,9... | collective-permute-start | bytes 1572872 | tf_op jit(solution)/shard_map/ppermute | solution.py:28
  26.8 0.9 shard_map.81
  27.7 0.9 shard_map.86.x_ref
  28.6 1.7 %collective-permute-done.5.y_ref = bf16[128,8,256]{2,1,0:T(8,128)(2,1)S(1)} collective-permute-done((bf16[128,8,256]{2,1,0:T(8,128)(2,1)S(1)}, bf16[128,8,256]{2,1,0:T(8,128)(2,1)S(1)}, u32[]{:S(2)}, u32[]{:S(2)}) %collective-permute-start.5) | collective-permute-done | bytes 524320 | tf_op jit(solution)/shard_map/ppermute | solution.py:28
  30.4 1.9 %collective-permute-start.6 = (bf16[128,8,256]{2,1,0:T(8,128)(2,1)S(1)}, bf16[128,8,256]{2,1,0:T(8,128)(2,1)S(1)}, u32[]{:S(2)}, u32[]{:S(2)}) collective-permute-start(bf16[128,8,256]{2,1,0:T(8,128)(2,1)S(1)} %shard_map.87), channel_id=1, source_target_pairs={{0,1},{1,2},{2,3},{3,4},{4,5},{5,6},{6,7},{7,0},{8,15},{9,8},{10,9... | collective-permute-start | bytes 1572872 | tf_op jit(solution)/shard_map/ppermute | solution.py:28
  32.4 4.7 %collective-permute-done.2 = bf16[128,8,256]{2,1,0:T(8,128)(2,1)S(1)} collective-permute-done((bf16[128,8,256]{2,1,0:T(8,128)(2,1)S(1)}, bf16[128,8,256]{2,1,0:T(8,128)(2,1)S(1)}, u32[]{:S(2)}, u32[]{:S(2)}) %collective-permute-start.2) | collective-permute-done | bytes 524320 | tf_op jit(solution)/shard_map/ppermute | solution.py:28
  37.2 1.9 %collective-permute-start.3 = (bf16[128,8,256]{2,1,0:T(8,128)(2,1)S(1)}, bf16[128,8,256]{2,1,0:T(8,128)(2,1)S(1)}, u32[]{:S(2)}, u32[]{:S(2)}) collective-permute-start(bf16[128,8,256]{2,1,0:T(8,128)(2,1)S(1)} %add_convert_fusion.3), channel_id=1, source_target_pairs={{0,1},{1,2},{2,3},{3,4},{4,5},{5,6},{6,7},{7,0},{8,15},{9,8},{10,9... | collective-permute-start | bytes 1572872 | tf_op jit(solution)/shard_map/ppermute | solution.py:28
  39.2 0.9 shard_map.80
  40.1 0.9 shard_map.85.x_ref
  41.0 1.7 %collective-permute-done.6.y_ref = bf16[128,8,256]{2,1,0:T(8,128)(2,1)S(1)} collective-permute-done((bf16[128,8,256]{2,1,0:T(8,128)(2,1)S(1)}, bf16[128,8,256]{2,1,0:T(8,128)(2,1)S(1)}, u32[]{:S(2)}, u32[]{:S(2)}) %collective-permute-start.6) | collective-permute-done | bytes 524320 | tf_op jit(solution)/shard_map/ppermute | solution.py:28
  42.9 1.9 %collective-permute-start.7 = (bf16[128,8,256]{2,1,0:T(8,128)(2,1)S(1)}, bf16[128,8,256]{2,1,0:T(8,128)(2,1)S(1)}, u32[]{:S(2)}, u32[]{:S(2)}) collective-permute-start(bf16[128,8,256]{2,1,0:T(8,128)(2,1)S(1)} %shard_map.88), channel_id=1, source_target_pairs={{0,9},{1,10},{2,11},{3,12},{4,13},{5,14},{6,15},{7,8},{8,7},{9,0},... | collective-permute-start | bytes 1572872 | tf_op jit(solution)/shard_map/ppermute | solution.py:28
  44.8 4.7 %collective-permute-done.3 = bf16[128,8,256]{2,1,0:T(8,128)(2,1)S(1)} collective-permute-done((bf16[128,8,256]{2,1,0:T(8,128)(2,1)S(1)}, bf16[128,8,256]{2,1,0:T(8,128)(2,1)S(1)}, u32[]{:S(2)}, u32[]{:S(2)}) %collective-permute-start.3) | collective-permute-done | bytes 524320 | tf_op jit(solution)/shard_map/ppermute | solution.py:28
  49.7 1.9 %collective-permute-start.4 = (bf16[128,8,256]{2,1,0:T(8,128)(2,1)S(1)}, bf16[128,8,256]{2,1,0:T(8,128)(2,1)S(1)}, u32[]{:S(2)}, u32[]{:S(2)}) collective-permute-start(bf16[128,8,256]{2,1,0:T(8,128)(2,1)S(1)} %add_convert_fusion.2), channel_id=1, source_target_pairs={{0,1},{1,2},{2,3},{3,4},{4,5},{5,6},{6,7},{7,0},{8,15},{9,8},{10,9... | collective-permute-start | bytes 1572872 | tf_op jit(solution)/shard_map/ppermute | solution.py:28
  51.6 0.9 shard_map.79
  52.5 0.8 collective-permute-done.7
  53.4 8.6 %collective-permute-done.4 = bf16[128,8,256]{2,1,0:T(8,128)(2,1)S(1)} collective-permute-done((bf16[128,8,256]{2,1,0:T(8,128)(2,1)S(1)}, bf16[128,8,256]{2,1,0:T(8,128)(2,1)S(1)}, u32[]{:S(2)}, u32[]{:S(2)}) %collective-permute-start.4) | collective-permute-done | bytes 524320 | tf_op jit(solution)/shard_map/ppermute | solution.py:28
  62.0 1.0 add_convert_fusion
  62.9 10.6 %all-to-all-start = ((bf16[64,2,8,256]{3,2,1,0:T(8,128)(2,1)}), bf16[64,2,8,256]{3,2,1,0:T(8,128)(2,1)S(1)}, u32[]{:S(2)}, u32[]{:S(2)}) async-start(bf16[64,2,8,256]{3,2,1,0:T(8,128)(2,1)} %bitcast.1), calls=%async_computation | async-start | bytes 1048576 | tf_op jit(solution)/shard_map/all_to_all | solution.py:255
  73.7 0.8 gather_fusion.1
  75.6 15.8 %all-to-all-done.got_ref = bf16[64,2,8,256]{3,2,1,0:T(8,128)(2,1)S(1)} async-done(((bf16[64,2,8,256]{3,2,1,0:T(8,128)(2,1)}), bf16[64,2,8,256]{3,2,1,0:T(8,128)(2,1)S(1)}, u32[]{:S(2)}, u32[]{:S(2)}) %all-to-all-start) | async-done | bytes 524320 | tf_op jit(solution)/shard_map/all_to_all | solution.py:255
  91.7 1.9 %collective-permute-start.8 = (bf16[512,256]{1,0:T(8,128)(2,1)S(1)}, bf16[512,256]{1,0:T(8,128)(2,1)S(1)}, u32[]{:S(2)}, u32[]{:S(2)}) collective-permute-start(bf16[512,256]{1,0:T(8,128)(2,1)S(1)} %shard_map.89.full_ref), channel_id=1, source_target_pairs={{0,8},{8,16},{16,24},{24,32},{32,40},{40,48},{48,56},{56,64},{64,7... | collective-permute-start | bytes 786440 | tf_op jit(solution)/shard_map/ppermute | solution.py:257
  93.6 1.5 %shard_map.90 = (bf16[1,256,256]{2,1,0:T(8,128)(2,1)}, bf16[256,512]{1,0:T(8,128)(2,1)S(1)}) custom-call(bf16[512,256]{1,0:T(8,128)(2,1)S(1)} %shard_map.89.full_ref, s32[1,4]{1,0:T(1,128)S(1)} %copy-done.3), custom_call_target="tpu_custom_call" | custom-call | flops 67108864 | bytes 1048576 | tf_op jit(solution)/shard_map/pallas_call | solution.py:167
  95.1 6.4 %collective-permute-done.8.near_ref = bf16[512,256]{1,0:T(8,128)(2,1)S(1)} collective-permute-done((bf16[512,256]{1,0:T(8,128)(2,1)S(1)}, bf16[512,256]{1,0:T(8,128)(2,1)S(1)}, u32[]{:S(2)}, u32[]{:S(2)}) %collective-permute-start.8) | collective-permute-done | bytes 262176 | tf_op jit(solution)/shard_map/ppermute | solution.py:257
  101.5 0.9 shard_map.91
  (28 shorter events, 2.2 us)
Async XLA Ops:
  0.6 74.1 %copy-start = (bf16[1,4096,128]{2,1,0:T(8,128)(2,1)S(1)}, bf16[1,4096,128]{2,1,0:T(8,128)(2,1)}, u32[]{:S(2)}) copy-start(bf16[1,4096,128]{2,1,0:T(8,128)(2,1)} %param.8) | copy-start | bytes 3145732
  0.6 10.0 %copy-start.2 = (bf16[512,1024]{1,0:T(8,128)(2,1)S(1)}, bf16[512,1024]{1,0:T(8,128)(2,1)}, u32[]{:S(2)}) copy-start(bf16[512,1024]{1,0:T(8,128)(2,1)} %occ_hbm.1) | copy-start | bytes 3145732
  0.7 3.8 %copy-start.1 = (bf16[8,256,512]{2,1,0:T(8,128)(2,1)S(1)}, bf16[8,256,512]{2,1,0:T(8,128)(2,1)}, u32[]{:S(2)}) copy-start(bf16[8,256,512]{2,1,0:T(8,128)(2,1)} %param.6) | copy-start | bytes 6291460
  4.5 7.7 %collective-permute-start.1 = (bf16[2048,512]{1,0:T(8,128)(2,1)S(1)}, bf16[2048,512]{1,0:T(8,128)(2,1)S(1)}, u32[]{:S(2)}, u32[]{:S(2)}) collective-permute-start(bf16[2048,512]{1,0:T(8,128)(2,1)S(1)} %bitcast.8), channel_id=1, source_target_pairs={{0,8},{8,0},{16,24},{24,16},{32,40},{40,32},{48,56},{56,48},{64,72... | collective-permute-start | bytes 6291464 | tf_op jit(solution)/shard_map/ppermute | solution.py:32
  6.4 18.3 %collective-permute-start = (bf16[128,8,256]{2,1,0:T(8,128)(2,1)}, bf16[128,8,256]{2,1,0:T(8,128)(2,1)S(1)}, u32[]{:S(2)}, u32[]{:S(2)}) collective-permute-start(bf16[128,8,256]{2,1,0:T(8,128)(2,1)} %shard_map.78), channel_id=1, source_target_pairs={{0,1},{1,2},{2,3},{3,4},{4,5},{5,6},{6,7},{7,0},{8,15},{9,8},{10,9... | collective-permute-start | bytes 1572872 | tf_op jit(solution)/shard_map/ppermute | solution.py:28
  13.1 17.2 %collective-permute-start.5 = (bf16[128,8,256]{2,1,0:T(8,128)(2,1)S(1)}, bf16[128,8,256]{2,1,0:T(8,128)(2,1)S(1)}, u32[]{:S(2)}, u32[]{:S(2)}) collective-permute-start(bf16[128,8,256]{2,1,0:T(8,128)(2,1)S(1)} %shard_map.83.after_ref), channel_id=1, source_target_pairs={{0,1},{1,2},{2,3},{3,4},{4,5},{5,6},{6,7},{7,0},{8,15},{9,8},{10,9... | collective-permute-start | bytes 1572872 | tf_op jit(solution)/shard_map/ppermute | solution.py:28
  24.8 12.3 %collective-permute-start.2 = (bf16[128,8,256]{2,1,0:T(8,128)(2,1)S(1)}, bf16[128,8,256]{2,1,0:T(8,128)(2,1)S(1)}, u32[]{:S(2)}, u32[]{:S(2)}) collective-permute-start(bf16[128,8,256]{2,1,0:T(8,128)(2,1)S(1)} %shard_map.84), channel_id=1, source_target_pairs={{0,1},{1,2},{2,3},{3,4},{4,5},{5,6},{6,7},{7,0},{8,15},{9,8},{10,9... | collective-permute-start | bytes 1572872 | tf_op jit(solution)/shard_map/ppermute | solution.py:28
  30.4 12.3 %collective-permute-start.6 = (bf16[128,8,256]{2,1,0:T(8,128)(2,1)S(1)}, bf16[128,8,256]{2,1,0:T(8,128)(2,1)S(1)}, u32[]{:S(2)}, u32[]{:S(2)}) collective-permute-start(bf16[128,8,256]{2,1,0:T(8,128)(2,1)S(1)} %shard_map.87), channel_id=1, source_target_pairs={{0,1},{1,2},{2,3},{3,4},{4,5},{5,6},{6,7},{7,0},{8,15},{9,8},{10,9... | collective-permute-start | bytes 1572872 | tf_op jit(solution)/shard_map/ppermute | solution.py:28
  37.2 12.3 %collective-permute-start.3 = (bf16[128,8,256]{2,1,0:T(8,128)(2,1)S(1)}, bf16[128,8,256]{2,1,0:T(8,128)(2,1)S(1)}, u32[]{:S(2)}, u32[]{:S(2)}) collective-permute-start(bf16[128,8,256]{2,1,0:T(8,128)(2,1)S(1)} %add_convert_fusion.3), channel_id=1, source_target_pairs={{0,1},{1,2},{2,3},{3,4},{4,5},{5,6},{6,7},{7,0},{8,15},{9,8},{10,9... | collective-permute-start | bytes 1572872 | tf_op jit(solution)/shard_map/ppermute | solution.py:28
  42.9 10.5 %collective-permute-start.7 = (bf16[128,8,256]{2,1,0:T(8,128)(2,1)S(1)}, bf16[128,8,256]{2,1,0:T(8,128)(2,1)S(1)}, u32[]{:S(2)}, u32[]{:S(2)}) collective-permute-start(bf16[128,8,256]{2,1,0:T(8,128)(2,1)S(1)} %shard_map.88), channel_id=1, source_target_pairs={{0,9},{1,10},{2,11},{3,12},{4,13},{5,14},{6,15},{7,8},{8,7},{9,0},... | collective-permute-start | bytes 1572872 | tf_op jit(solution)/shard_map/ppermute | solution.py:28
  49.7 12.3 %collective-permute-start.4 = (bf16[128,8,256]{2,1,0:T(8,128)(2,1)S(1)}, bf16[128,8,256]{2,1,0:T(8,128)(2,1)S(1)}, u32[]{:S(2)}, u32[]{:S(2)}) collective-permute-start(bf16[128,8,256]{2,1,0:T(8,128)(2,1)S(1)} %add_convert_fusion.2), channel_id=1, source_target_pairs={{0,1},{1,2},{2,3},{3,4},{4,5},{5,6},{6,7},{7,0},{8,15},{9,8},{10,9... | collective-permute-start | bytes 1572872 | tf_op jit(solution)/shard_map/ppermute | solution.py:28
  52.5 21.0 %copy-start.4 = (s32[4,16]{1,0:T(4,128)S(1)}, s32[4,16]{1,0:T(4,128)}, u32[]{:S(2)}) copy-start(s32[4,16]{1,0:T(4,128)} %param.11) | copy-start | bytes 772
  52.5 21.1 %copy-start.5 = (s32[1,256]{1,0:T(1,128)S(1)}, s32[1,256]{1,0:T(1,128)}, u32[]{:S(2)}) copy-start(s32[1,256]{1,0:T(1,128)} %param.9) | copy-start | bytes 3076
  62.9 30.7 %copy-start.3 = (s32[1,4]{1,0:T(1,128)S(1)}, s32[1,4]{1,0:T(1,128)}, u32[]{:S(2)}) copy-start(s32[1,4]{1,0:T(1,128)} %keep_ref.1) | copy-start | bytes 52
  62.9 28.4 %all-to-all-start = ((bf16[64,2,8,256]{3,2,1,0:T(8,128)(2,1)}), bf16[64,2,8,256]{3,2,1,0:T(8,128)(2,1)S(1)}, u32[]{:S(2)}, u32[]{:S(2)}) async-start(bf16[64,2,8,256]{3,2,1,0:T(8,128)(2,1)} %bitcast.1), calls=%async_computation | async-start | bytes 1048576 | tf_op jit(solution)/shard_map/all_to_all | solution.py:255
  91.7 9.8 %collective-permute-start.8 = (bf16[512,256]{1,0:T(8,128)(2,1)S(1)}, bf16[512,256]{1,0:T(8,128)(2,1)S(1)}, u32[]{:S(2)}, u32[]{:S(2)}) collective-permute-start(bf16[512,256]{1,0:T(8,128)(2,1)S(1)} %shard_map.89.full_ref), channel_id=1, source_target_pairs={{0,8},{8,16},{16,24},{24,32},{32,40},{40,48},{48,56},{56,64},{64,7... | collective-permute-start | bytes 786440 | tf_op jit(solution)/shard_map/ppermute | solution.py:257

commit v5 on v4

--- a/solution.py
+++ b/solution.py
@@ -239,12 +239,13 @@
         own = [hop(v, doms, ring) for v in own]
         if i == 0:
             own = [after_add(t, v, o) for t, v, o in zip(term(w, i, slab, aux_rows), own, other)]
-        else:
+        elif i < half_ring - 1:
             own = [add(t, v) for t, v in zip(term(w, i, slab, aux_rows), own)]
         if i < half_ring - 1:
             if i > 0:
                 other = [steer_add(t, v, HINT_B) for t, v in zip(term(w, i, other_slab, aux_rows), other)]
             other = [hop(v, doms, ring, 1 if i == half_ring - 2 else 0) for v in other]
+    other = [steer_add(t, o, HINT_B) for t, o in zip(term(w, half_ring - 1, slab, aux_rows), other)]
     halves = [add(v, o) for v, o in zip(own, other)]
 
     shells = pao_coef[0].reshape(-1, AOB, pao_d)

time: 103 us -> 103 us (level)
  transfers between devices with their start and end apart: 10 -> 10, of which waited for: 9 -> 9; matrix products, arithmetic and copies ran while one was open for 2% -> 2% of each run, Pallas kernels for 9% -> 10%
where the time goes in v5:
time: 103 us; the launch traced here: 102 us
  waiting for transfers between devices  50.8 us (49%)
  starting transfers between devices  32.6 us (32%)
  Pallas kernels  14.8 us (14%)
  local copies, waits for them, and re-layouts  1.79 us (2%)
  other arithmetic  1.43 us (1%)
    ppermute x7, waiting for transfers between devices, hop(): return lax.ppermute(value, ('dom', 'ao'), pairs)  28.6 us
    ppermute x7, starting transfers between devices, hop(): return lax.ppermute(value, ('dom', 'ao'), pairs)  18.2 us
    all_to_all x1, waiting for transfers between devices, body(): got = lax.all_to_all(half, 'dom', split_axis=0, concat_axis=0, tiled=True)  15.8 us
    all_to_all x1, starting transfers between devices, body(): got = lax.all_to_all(half, 'dom', split_axis=0, concat_axis=0, tiled=True)  10.6 us
    ppermute x1, waiting for transfers between devices, body(): near = lax.ppermute(full, 'dom', [(d, (d + 1) % doms) for d in range(doms)])  6.36 us
    pallas_call x7, Pallas kernels, term(): pl.pallas_call(term_kernel, grid=(1,), out_shape=[jax.ShapeDtypeStruct((r...  6.35 us
    pallas_call x1, Pallas kernels, first_term(): pl.pallas_call(functools.partial(first_kernel, ring), out_shape=[jax.Shap...  3.77 us
  transfers between devices with their start and end apart: 10, of which 9 were waited for; matrix products, arithmetic and copies ran while one was open for 2% of the time, Pallas kernels for 10%

profile of v5, /device:TPU:16, one launch (start us, length us, event | category | flops | bytes accessed | tf_op | source)
XLA Modules:
  0.0 102.3 jit_solution(12751871126732884578)
XLA Ops:
  0.7 3.8 %shard_map.78 = bf16[128,8,256]{2,1,0:T(8,128)(2,1)} custom-call(bf16[512,1024]{1,0:T(8,128)(2,1)} %occ_hbm.1, bf16[2048,512]{1,0:T(8,128)(2,1)} %bitcast.7), custom_call_target="tpu_custom_call" | custom-call | flops 268435456 | bytes 3145728 | tf_op jit(solution)/shard_map/pallas_call | solution.py:70
  4.5 1.9 %collective-permute-start.1 = (bf16[2048,512]{1,0:T(8,128)(2,1)S(1)}, bf16[2048,512]{1,0:T(8,128)(2,1)S(1)}, u32[]{:S(2)}, u32[]{:S(2)}) collective-permute-start(bf16[2048,512]{1,0:T(8,128)(2,1)S(1)} %bitcast.8), channel_id=1, source_target_pairs={{0,8},{8,0},{16,24},{24,16},{32,40},{40,32},{48,56},{56,48},{64,72... | collective-permute-start | bytes 6291464 | tf_op jit(solution)/shard_map/ppermute | solution.py:32
  6.4 4.3 %collective-permute-start = (bf16[128,8,256]{2,1,0:T(8,128)(2,1)}, bf16[128,8,256]{2,1,0:T(8,128)(2,1)S(1)}, u32[]{:S(2)}, u32[]{:S(2)}) collective-permute-start(bf16[128,8,256]{2,1,0:T(8,128)(2,1)} %shard_map.78), channel_id=1, source_target_pairs={{0,1},{1,2},{2,3},{3,4},{4,5},{5,6},{6,7},{7,0},{8,15},{9,8},{10,9... | collective-permute-start | bytes 1572872 | tf_op jit(solution)/shard_map/ppermute | solution.py:28
  10.7 1.5 %shard_map.77.w_ref = bf16[4,128,512]{2,1,0:T(8,128)(2,1)S(1)} custom-call(bf16[512,1024]{1,0:T(8,128)(2,1)S(1)} %copy-done.2), custom_call_target="tpu_custom_call" | custom-call | flops 536870912 | bytes 2097152 | tf_op jit(solution)/shard_map/pallas_call | solution.py:94
  12.2 0.9 shard_map.82.after_ref
  13.1 4.3 %collective-permute-start.5 = (bf16[128,8,256]{2,1,0:T(8,128)(2,1)S(1)}, bf16[128,8,256]{2,1,0:T(8,128)(2,1)S(1)}, u32[]{:S(2)}, u32[]{:S(2)}) collective-permute-start(bf16[128,8,256]{2,1,0:T(8,128)(2,1)S(1)} %shard_map.82.after_ref), channel_id=1, source_target_pairs={{0,1},{1,2},{2,3},{3,4},{4,5},{5,6},{6,7},{7,0},{8,15},{9,8},{10,9... | collective-permute-start | bytes 1572872 | tf_op jit(solution)/shard_map/ppermute | solution.py:28
  17.4 0.9 shard_map.81.x_ref
  18.3 6.4 %collective-permute-done.y_ref = bf16[128,8,256]{2,1,0:T(8,128)(2,1)S(1)} collective-permute-done((bf16[128,8,256]{2,1,0:T(8,128)(2,1)}, bf16[128,8,256]{2,1,0:T(8,128)(2,1)S(1)}, u32[]{:S(2)}, u32[]{:S(2)}) %collective-permute-start) | collective-permute-done | bytes 524320 | tf_op jit(solution)/shard_map/ppermute | solution.py:28
  24.8 1.9 %collective-permute-start.2 = (bf16[128,8,256]{2,1,0:T(8,128)(2,1)S(1)}, bf16[128,8,256]{2,1,0:T(8,128)(2,1)S(1)}, u32[]{:S(2)}, u32[]{:S(2)}) collective-permute-start(bf16[128,8,256]{2,1,0:T(8,128)(2,1)S(1)} %shard_map.83), channel_id=1, source_target_pairs={{0,1},{1,2},{2,3},{3,4},{4,5},{5,6},{6,7},{7,0},{8,15},{9,8},{10,9... | collective-permute-start | bytes 1572872 | tf_op jit(solution)/shard_map/ppermute | solution.py:28
  26.7 0.9 shard_map.80
  27.7 0.9 shard_map.86.x_ref
  28.6 1.7 %collective-permute-done.5.y_ref = bf16[128,8,256]{2,1,0:T(8,128)(2,1)S(1)} collective-permute-done((bf16[128,8,256]{2,1,0:T(8,128)(2,1)S(1)}, bf16[128,8,256]{2,1,0:T(8,128)(2,1)S(1)}, u32[]{:S(2)}, u32[]{:S(2)}) %collective-permute-start.5) | collective-permute-done | bytes 524320 | tf_op jit(solution)/shard_map/ppermute | solution.py:28
  30.4 1.9 %collective-permute-start.6 = (bf16[128,8,256]{2,1,0:T(8,128)(2,1)S(1)}, bf16[128,8,256]{2,1,0:T(8,128)(2,1)S(1)}, u32[]{:S(2)}, u32[]{:S(2)}) collective-permute-start(bf16[128,8,256]{2,1,0:T(8,128)(2,1)S(1)} %shard_map.87), channel_id=1, source_target_pairs={{0,1},{1,2},{2,3},{3,4},{4,5},{5,6},{6,7},{7,0},{8,15},{9,8},{10,9... | collective-permute-start | bytes 1572872 | tf_op jit(solution)/shard_map/ppermute | solution.py:28
  32.4 4.7 %collective-permute-done.2 = bf16[128,8,256]{2,1,0:T(8,128)(2,1)S(1)} collective-permute-done((bf16[128,8,256]{2,1,0:T(8,128)(2,1)S(1)}, bf16[128,8,256]{2,1,0:T(8,128)(2,1)S(1)}, u32[]{:S(2)}, u32[]{:S(2)}) %collective-permute-start.2) | collective-permute-done | bytes 524320 | tf_op jit(solution)/shard_map/ppermute | solution.py:28
  37.2 1.9 %collective-permute-start.3 = (bf16[128,8,256]{2,1,0:T(8,128)(2,1)S(1)}, bf16[128,8,256]{2,1,0:T(8,128)(2,1)S(1)}, u32[]{:S(2)}, u32[]{:S(2)}) collective-permute-start(bf16[128,8,256]{2,1,0:T(8,128)(2,1)S(1)} %add_convert_fusion.2), channel_id=1, source_target_pairs={{0,1},{1,2},{2,3},{3,4},{4,5},{5,6},{6,7},{7,0},{8,15},{9,8},{10,9... | collective-permute-start | bytes 1572872 | tf_op jit(solution)/shard_map/ppermute | solution.py:28
  39.2 0.9 shard_map.79
  40.1 0.9 shard_map.85.x_ref
  41.0 1.7 %collective-permute-done.6.y_ref = bf16[128,8,256]{2,1,0:T(8,128)(2,1)S(1)} collective-permute-done((bf16[128,8,256]{2,1,0:T(8,128)(2,1)S(1)}, bf16[128,8,256]{2,1,0:T(8,128)(2,1)S(1)}, u32[]{:S(2)}, u32[]{:S(2)}) %collective-permute-start.6) | collective-permute-done | bytes 524320 | tf_op jit(solution)/shard_map/ppermute | solution.py:28
  42.8 1.9 %collective-permute-start.7 = (bf16[128,8,256]{2,1,0:T(8,128)(2,1)S(1)}, bf16[128,8,256]{2,1,0:T(8,128)(2,1)S(1)}, u32[]{:S(2)}, u32[]{:S(2)}) collective-permute-start(bf16[128,8,256]{2,1,0:T(8,128)(2,1)S(1)} %shard_map.88), channel_id=1, source_target_pairs={{0,9},{1,10},{2,11},{3,12},{4,13},{5,14},{6,15},{7,8},{8,7},{9,0},... | collective-permute-start | bytes 1572872 | tf_op jit(solution)/shard_map/ppermute | solution.py:28
  44.8 4.7 %collective-permute-done.3 = bf16[128,8,256]{2,1,0:T(8,128)(2,1)S(1)} collective-permute-done((bf16[128,8,256]{2,1,0:T(8,128)(2,1)S(1)}, bf16[128,8,256]{2,1,0:T(8,128)(2,1)S(1)}, u32[]{:S(2)}, u32[]{:S(2)}) %collective-permute-start.3) | collective-permute-done | bytes 524320 | tf_op jit(solution)/shard_map/ppermute | solution.py:28
  49.7 1.9 %collective-permute-start.4 = (bf16[128,8,256]{2,1,0:T(8,128)(2,1)S(1)}, bf16[128,8,256]{2,1,0:T(8,128)(2,1)S(1)}, u32[]{:S(2)}, u32[]{:S(2)}) collective-permute-start(bf16[128,8,256]{2,1,0:T(8,128)(2,1)S(1)} %add_convert_fusion.1), channel_id=1, source_target_pairs={{0,1},{1,2},{2,3},{3,4},{4,5},{5,6},{6,7},{7,0},{8,15},{9,8},{10,9... | collective-permute-start | bytes 1572872 | tf_op jit(solution)/shard_map/ppermute | solution.py:28
  51.6 0.9 shard_map.84.x_ref
  52.5 0.8 collective-permute-done.7.y_ref
  53.5 8.5 %collective-permute-done.4 = bf16[128,8,256]{2,1,0:T(8,128)(2,1)S(1)} collective-permute-done((bf16[128,8,256]{2,1,0:T(8,128)(2,1)S(1)}, bf16[128,8,256]{2,1,0:T(8,128)(2,1)S(1)}, u32[]{:S(2)}, u32[]{:S(2)}) %collective-permute-start.4) | collective-permute-done | bytes 524320 | tf_op jit(solution)/shard_map/ppermute | solution.py:28
  61.9 0.9 add_convert_fusion
  62.9 10.6 %all-to-all-start = ((bf16[64,2,8,256]{3,2,1,0:T(8,128)(2,1)}), bf16[64,2,8,256]{3,2,1,0:T(8,128)(2,1)S(1)}, u32[]{:S(2)}, u32[]{:S(2)}) async-start(bf16[64,2,8,256]{3,2,1,0:T(8,128)(2,1)} %bitcast.1), calls=%async_computation | async-start | bytes 1048576 | tf_op jit(solution)/shard_map/all_to_all | solution.py:256
  74.2 0.8 gather_fusion.1
  75.5 15.8 %all-to-all-done.got_ref = bf16[64,2,8,256]{3,2,1,0:T(8,128)(2,1)S(1)} async-done(((bf16[64,2,8,256]{3,2,1,0:T(8,128)(2,1)}), bf16[64,2,8,256]{3,2,1,0:T(8,128)(2,1)S(1)}, u32[]{:S(2)}, u32[]{:S(2)}) %all-to-all-start) | async-done | bytes 524320 | tf_op jit(solution)/shard_map/all_to_all | solution.py:256
  91.6 1.9 %collective-permute-start.8 = (bf16[512,256]{1,0:T(8,128)(2,1)S(1)}, bf16[512,256]{1,0:T(8,128)(2,1)S(1)}, u32[]{:S(2)}, u32[]{:S(2)}) collective-permute-start(bf16[512,256]{1,0:T(8,128)(2,1)S(1)} %shard_map.90.full_ref), channel_id=1, source_target_pairs={{0,8},{8,16},{16,24},{24,32},{32,40},{40,48},{48,56},{56,64},{64,7... | collective-permute-start | bytes 786440 | tf_op jit(solution)/shard_map/ppermute | solution.py:258
  93.5 1.5 %shard_map.91 = (bf16[1,256,256]{2,1,0:T(8,128)(2,1)}, bf16[256,512]{1,0:T(8,128)(2,1)S(1)}) custom-call(bf16[512,256]{1,0:T(8,128)(2,1)S(1)} %shard_map.90.full_ref, s32[1,4]{1,0:T(1,128)S(1)} %copy-done.3), custom_call_target="tpu_custom_call" | custom-call | flops 67108864 | bytes 1048576 | tf_op jit(solution)/shard_map/pallas_call | solution.py:167
  95.0 6.4 %collective-permute-done.8.near_ref = bf16[512,256]{1,0:T(8,128)(2,1)S(1)} collective-permute-done((bf16[512,256]{1,0:T(8,128)(2,1)S(1)}, bf16[512,256]{1,0:T(8,128)(2,1)S(1)}, u32[]{:S(2)}, u32[]{:S(2)}) %collective-permute-start.8) | collective-permute-done | bytes 262176 | tf_op jit(solution)/shard_map/ppermute | solution.py:258
  101.4 0.9 shard_map.92
  (29 shorter events, 2.3 us)
Async XLA Ops:
  0.6 72.9 %copy-start = (bf16[1,4096,128]{2,1,0:T(8,128)(2,1)S(1)}, bf16[1,4096,128]{2,1,0:T(8,128)(2,1)}, u32[]{:S(2)}) copy-start(bf16[1,4096,128]{2,1,0:T(8,128)(2,1)} %param.8) | copy-start | bytes 3145732
  0.6 3.8 %copy-start.1 = (bf16[8,256,512]{2,1,0:T(8,128)(2,1)S(1)}, bf16[8,256,512]{2,1,0:T(8,128)(2,1)}, u32[]{:S(2)}) copy-start(bf16[8,256,512]{2,1,0:T(8,128)(2,1)} %param.6) | copy-start | bytes 6291460
  0.7 10.0 %copy-start.2 = (bf16[512,1024]{1,0:T(8,128)(2,1)S(1)}, bf16[512,1024]{1,0:T(8,128)(2,1)}, u32[]{:S(2)}) copy-start(bf16[512,1024]{1,0:T(8,128)(2,1)} %occ_hbm.1) | copy-start | bytes 3145732
  4.5 7.7 %collective-permute-start.1 = (bf16[2048,512]{1,0:T(8,128)(2,1)S(1)}, bf16[2048,512]{1,0:T(8,128)(2,1)S(1)}, u32[]{:S(2)}, u32[]{:S(2)}) collective-permute-start(bf16[2048,512]{1,0:T(8,128)(2,1)S(1)} %bitcast.8), channel_id=1, source_target_pairs={{0,8},{8,0},{16,24},{24,16},{32,40},{40,32},{48,56},{56,48},{64,72... | collective-permute-start | bytes 6291464 | tf_op jit(solution)/shard_map/ppermute | solution.py:32
  6.4 18.3 %collective-permute-start = (bf16[128,8,256]{2,1,0:T(8,128)(2,1)}, bf16[128,8,256]{2,1,0:T(8,128)(2,1)S(1)}, u32[]{:S(2)}, u32[]{:S(2)}) collective-permute-start(bf16[128,8,256]{2,1,0:T(8,128)(2,1)} %shard_map.78), channel_id=1, source_target_pairs={{0,1},{1,2},{2,3},{3,4},{4,5},{5,6},{6,7},{7,0},{8,15},{9,8},{10,9... | collective-permute-start | bytes 1572872 | tf_op jit(solution)/shard_map/ppermute | solution.py:28
  13.1 17.2 %collective-permute-start.5 = (bf16[128,8,256]{2,1,0:T(8,128)(2,1)S(1)}, bf16[128,8,256]{2,1,0:T(8,128)(2,1)S(1)}, u32[]{:S(2)}, u32[]{:S(2)}) collective-permute-start(bf16[128,8,256]{2,1,0:T(8,128)(2,1)S(1)} %shard_map.82.after_ref), channel_id=1, source_target_pairs={{0,1},{1,2},{2,3},{3,4},{4,5},{5,6},{6,7},{7,0},{8,15},{9,8},{10,9... | collective-permute-start | bytes 1572872 | tf_op jit(solution)/shard_map/ppermute | solution.py:28
  24.8 12.3 %collective-permute-start.2 = (bf16[128,8,256]{2,1,0:T(8,128)(2,1)S(1)}, bf16[128,8,256]{2,1,0:T(8,128)(2,1)S(1)}, u32[]{:S(2)}, u32[]{:S(2)}) collective-permute-start(bf16[128,8,256]{2,1,0:T(8,128)(2,1)S(1)} %shard_map.83), channel_id=1, source_target_pairs={{0,1},{1,2},{2,3},{3,4},{4,5},{5,6},{6,7},{7,0},{8,15},{9,8},{10,9... | collective-permute-start | bytes 1572872 | tf_op jit(solution)/shard_map/ppermute | solution.py:28
  30.4 12.3 %collective-permute-start.6 = (bf16[128,8,256]{2,1,0:T(8,128)(2,1)S(1)}, bf16[128,8,256]{2,1,0:T(8,128)(2,1)S(1)}, u32[]{:S(2)}, u32[]{:S(2)}) collective-permute-start(bf16[128,8,256]{2,1,0:T(8,128)(2,1)S(1)} %shard_map.87), channel_id=1, source_target_pairs={{0,1},{1,2},{2,3},{3,4},{4,5},{5,6},{6,7},{7,0},{8,15},{9,8},{10,9... | collective-permute-start | bytes 1572872 | tf_op jit(solution)/shard_map/ppermute | solution.py:28
  37.2 12.3 %collective-permute-start.3 = (bf16[128,8,256]{2,1,0:T(8,128)(2,1)S(1)}, bf16[128,8,256]{2,1,0:T(8,128)(2,1)S(1)}, u32[]{:S(2)}, u32[]{:S(2)}) collective-permute-start(bf16[128,8,256]{2,1,0:T(8,128)(2,1)S(1)} %add_convert_fusion.2), channel_id=1, source_target_pairs={{0,1},{1,2},{2,3},{3,4},{4,5},{5,6},{6,7},{7,0},{8,15},{9,8},{10,9... | collective-permute-start | bytes 1572872 | tf_op jit(solution)/shard_map/ppermute | solution.py:28
  42.8 10.5 %collective-permute-start.7 = (bf16[128,8,256]{2,1,0:T(8,128)(2,1)S(1)}, bf16[128,8,256]{2,1,0:T(8,128)(2,1)S(1)}, u32[]{:S(2)}, u32[]{:S(2)}) collective-permute-start(bf16[128,8,256]{2,1,0:T(8,128)(2,1)S(1)} %shard_map.88), channel_id=1, source_target_pairs={{0,9},{1,10},{2,11},{3,12},{4,13},{5,14},{6,15},{7,8},{8,7},{9,0},... | collective-permute-start | bytes 1572872 | tf_op jit(solution)/shard_map/ppermute | solution.py:28
  49.7 12.3 %collective-permute-start.4 = (bf16[128,8,256]{2,1,0:T(8,128)(2,1)S(1)}, bf16[128,8,256]{2,1,0:T(8,128)(2,1)S(1)}, u32[]{:S(2)}, u32[]{:S(2)}) collective-permute-start(bf16[128,8,256]{2,1,0:T(8,128)(2,1)S(1)} %add_convert_fusion.1), channel_id=1, source_target_pairs={{0,1},{1,2},{2,3},{3,4},{4,5},{5,6},{6,7},{7,0},{8,15},{9,8},{10,9... | collective-permute-start | bytes 1572872 | tf_op jit(solution)/shard_map/ppermute | solution.py:28
  52.5 21.0 %copy-start.4 = (s32[4,16]{1,0:T(4,128)S(1)}, s32[4,16]{1,0:T(4,128)}, u32[]{:S(2)}) copy-start(s32[4,16]{1,0:T(4,128)} %param.11) | copy-start | bytes 772
  52.5 21.7 %copy-start.5 = (s32[1,256]{1,0:T(1,128)S(1)}, s32[1,256]{1,0:T(1,128)}, u32[]{:S(2)}) copy-start(s32[1,256]{1,0:T(1,128)} %param.9) | copy-start | bytes 3076
  62.9 30.7 %copy-start.3 = (s32[1,4]{1,0:T(1,128)S(1)}, s32[1,4]{1,0:T(1,128)}, u32[]{:S(2)}) copy-start(s32[1,4]{1,0:T(1,128)} %keep_ref.1) | copy-start | bytes 52
  62.9 28.4 %all-to-all-start = ((bf16[64,2,8,256]{3,2,1,0:T(8,128)(2,1)}), bf16[64,2,8,256]{3,2,1,0:T(8,128)(2,1)S(1)}, u32[]{:S(2)}, u32[]{:S(2)}) async-start(bf16[64,2,8,256]{3,2,1,0:T(8,128)(2,1)} %bitcast.1), calls=%async_computation | async-start | bytes 1048576 | tf_op jit(solution)/shard_map/all_to_all | solution.py:256
  91.6 9.8 %collective-permute-start.8 = (bf16[512,256]{1,0:T(8,128)(2,1)S(1)}, bf16[512,256]{1,0:T(8,128)(2,1)S(1)}, u32[]{:S(2)}, u32[]{:S(2)}) collective-permute-start(bf16[512,256]{1,0:T(8,128)(2,1)S(1)} %shard_map.90.full_ref), channel_id=1, source_target_pairs={{0,8},{8,16},{16,24},{24,32},{32,40},{40,48},{48,56},{56,64},{64,7... | collective-permute-start | bytes 786440 | tf_op jit(solution)/shard_map/ppermute | solution.py:258
